TPU v7x, 128 devices: a whole 4x4x4 slice. The times are simulated.
128 devices in a mesh: gx: 64 (over z, x_lo, y, core), col: 2 (over x_hi).
Axes of the slice: x: 4 (x_hi: 2, x_lo: 2; x = x_hi * 2 + x_lo), y: 4, z: 4, core: 2. Of those that a mesh axis runs over, the one named last changes fastest.
Arguments:
- state_field: bfloat16 [1024, 64, 8192], P('gx', 'col'), may hold values from -6 to 6
- spectral_weight: bfloat16 [2, 64, 64, 8192], P(None, None, 'col', 'gx'), may hold values from -0.75 to 0.75
- local_weight: float32 [64], P('col'), may hold values from 0.5 to 1.5
- channel_bias: float32 [64], P('col'), may hold values from -3 to 3
Outputs:
- layer_out: bfloat16 [1024, 64, 8192], P('gx', 'col')
All inputs are finite; a program needn't handle non-finite values.
Results may differ from a plain program's by a relative error of at most 0.0085.
Values may be sent and summed in bfloat16 or wider, within the bound.
A program may use at most 128 MiB of HBM per device.

v0:
```python
from functools import partial
import math

import jax
import jax.numpy as jnp
from jax import lax
from jax.sharding import PartitionSpec as P

YCELLS = 128
TSTEPS = 64
KX = 32
KY = 32
KT = 8


def frequencies(number_modes):
    positions = jnp.arange(number_modes, dtype=jnp.int32)
    return jnp.where(positions < number_modes // 2, positions, positions - number_modes)


def yt_tables():
    y_index = jnp.arange(YCELLS, dtype=jnp.int32)
    t_index = jnp.arange(TSTEPS, dtype=jnp.int32)
    y_freq = frequencies(KY)
    t_freq = jnp.arange(KT, dtype=jnp.int32)
    phases = (
        y_index[:, None, None, None] * y_freq[None, None, :, None] * TSTEPS
        + t_index[None, :, None, None] * t_freq[None, None, None, :] * YCELLS
    ) % (YCELLS * TSTEPS)
    phases = phases.reshape(YCELLS * TSTEPS, KY * KT)
    angles = phases.astype(jnp.float32) * (2.0 * math.pi / (YCELLS * TSTEPS))
    cosine_table = jnp.cos(angles)
    sine_table = jnp.sin(angles)
    time_weights = jnp.tile(jnp.where(t_freq == 0, 1.0, 2.0).astype(jnp.float32), KY)
    forward_table = jnp.concatenate([cosine_table, -sine_table], axis=1).astype(jnp.bfloat16)
    inverse_table = jnp.concatenate(
        [time_weights * cosine_table, -time_weights * sine_table], axis=1
    ).T.astype(jnp.bfloat16)
    return (forward_table, inverse_table)


def x_tables(positions, period):
    phases = positions[:, None] * frequencies(KX)[None, :] % period
    angles = phases.astype(jnp.float32) * (2.0 * math.pi / period)
    return (jnp.cos(angles), jnp.sin(angles))


def forward_x(spectra, cosine_table, sine_table):
    einsum_high = partial(jnp.einsum, precision=lax.Precision.HIGHEST)
    real_part = spectra[:, :, 0]
    imag_part = spectra[:, :, 1]
    out_real = einsum_high("xck,xm->ckm", real_part, cosine_table) + einsum_high(
        "xck,xm->ckm", imag_part, sine_table
    )
    out_imag = einsum_high("xck,xm->ckm", imag_part, cosine_table) - einsum_high(
        "xck,xm->ckm", real_part, sine_table
    )
    return jnp.stack([out_real, out_imag], axis=1)


def inverse_x(mode_values, cosine_table, sine_table):
    einsum_high = partial(jnp.einsum, precision=lax.Precision.HIGHEST)
    real_part = mode_values[:, 0]
    imag_part = mode_values[:, 1]
    out_real = einsum_high("ckm,xm->xck", real_part, cosine_table) - einsum_high(
        "ckm,xm->xck", imag_part, sine_table
    )
    out_imag = einsum_high("ckm,xm->xck", real_part, sine_table) + einsum_high(
        "ckm,xm->xck", imag_part, cosine_table
    )
    return jnp.stack([out_real, out_imag], axis=2)


def mix_modes(mode_values, weight):
    einsum_high = partial(jnp.einsum, precision=lax.Precision.HIGHEST)
    mode_real = mode_values[:, 0].astype(jnp.float32)
    mode_imag = mode_values[:, 1].astype(jnp.float32)
    weight_real = weight[0].astype(jnp.float32)
    weight_imag = weight[1].astype(jnp.float32)
    out_real = einsum_high("iom,im->om", weight_real, mode_real) - einsum_high(
        "iom,im->om", weight_imag, mode_imag
    )
    out_imag = einsum_high("iom,im->om", weight_real, mode_imag) + einsum_high(
        "iom,im->om", weight_imag, mode_real
    )
    return jnp.stack([out_real, out_imag], axis=1)


def shards(state_field, spectral_weight, local_weight, channel_bias):
    slab_rows = state_field.shape[0]
    group_size = state_field.shape[1]
    plane_cells = state_field.shape[2]
    slab_count = lax.axis_size("gx")
    period = slab_rows * slab_count
    forward_table, inverse_table = yt_tables()
    spectra = jnp.dot(
        state_field.reshape(slab_rows * group_size, plane_cells),
        forward_table,
        preferred_element_type=jnp.float32,
    ).reshape(slab_rows, group_size, 2, KY * KT)
    forward_scale = 1.0 / math.sqrt(period * YCELLS * TSTEPS)
    local_positions = lax.axis_index("gx") * slab_rows + jnp.arange(slab_rows, dtype=jnp.int32)
    local_cosine, local_sine = x_tables(local_positions, period)
    partial_modes = (forward_x(spectra, local_cosine, local_sine) * forward_scale).reshape(
        group_size, 2, KY * KT * KX
    )
    owned_modes = lax.psum_scatter(partial_modes, "gx", scatter_dimension=2, tiled=True)
    owned_modes = owned_modes.astype(jnp.bfloat16)
    all_channels = lax.all_gather(owned_modes, "col", axis=0, tiled=True)
    mixed_local = mix_modes(all_channels, spectral_weight).astype(jnp.bfloat16)
    whole_modes = lax.all_gather(mixed_local, "gx", axis=2, tiled=True)
    whole_modes = whole_modes.astype(jnp.float32).reshape(group_size, 2, KY * KT, KX)
    slab_values = inverse_x(whole_modes, local_cosine, local_sine).astype(jnp.bfloat16)
    inverse_scale = 1.0 / math.sqrt(KX * KY * KT)
    spectral_out = (
        jnp.dot(
            slab_values.reshape(slab_rows * group_size, 2 * KY * KT),
            inverse_table,
            preferred_element_type=jnp.float32,
        )
        * inverse_scale
    )
    spectral_out = spectral_out.reshape(slab_rows, group_size, plane_cells)
    summed = (
        spectral_out
        + local_weight[None, :, None] * state_field.astype(jnp.float32)
        + channel_bias[None, :, None]
    )
    return jax.nn.gelu(summed, approximate=True).astype(jnp.bfloat16)


def solution(mesh):
    return jax.shard_map(
        shards,
        mesh=mesh,
        in_specs=(P("gx", "col", None), P(None, None, "col", "gx"), P("col"), P("col")),
        out_specs=P("gx", "col", None),
        check_vma=False,
    )
```

profile of v0, /device:TPU:1, one launch (start us, length us, event | category | flops | bytes accessed | tf_op | source)
XLA Modules:
  0.0 535.1 jit_solution(9548540661863798427)
XLA Ops:
  6.6 0.1 mul.222
  6.7 6.3 %broadcast_add_fusion = s32[128,64,32,8]{1,0,3,2:T(8,128)} fusion(s32[64,8]{0,1:T(8,128)S(1)} %multiply_multiply_fusion.2, s32[128,32]{0,1:T(8,128)S(1)} %multiply_multiply_fusion.1), kind=kLoop, calls=%fused_computation.26 | loop fusion | flops 2097152 | bytes 8407040 | tf_op jit(solution)/shard_map/add | solution.py:27
  13.1 14.7 %add.119 = s32[8192,256]{0,1:T(8,128)} reshape(s32[128,64,32,8]{1,0,3,2:T(8,128)} %broadcast_add_fusion) | data formatting | bytes 16777216 | tf_op jit(solution)/shard_map/add | solution.py:27
  27.8 36.3 %multiply_convert_fusion.1 = (bf16[8192,256]{0,1:T(8,128)(2,1)}, bf16[8192,256]{0,1:T(8,128)(2,1)}, bf16[8192,256]{0,1:T(8,128)(2,1)S(1)}, bf16[8192,256]{0,1:T(8,128)(2,1)S(1)}) fusion(f32[256]{0:T(256)S(1)} %mul.222, s32[8192,256]{0,1:T(8,128)} %add.119, f32[256]{0:T(256)S(1)} %neg.11), kind=kLoop, calls=%fused_computation.24 | loop fusion | flops 41943040 | bytes 25167872 | tf_op jit(solution)/shard_map/convert
  64.1 7.9 %fusion.25 = f32[512,512]{0,1:T(8,128)S(1)} fusion(bf16[512,8192]{1,0:T(8,128)(2,1)} %bitcast.108, bf16[8192,256]{0,1:T(8,128)(2,1)S(1)} %get-tuple-element.13, bf16[8192,256]{0,1:T(8,128)(2,1)S(1)} %get-tuple-element.14), kind=kOutput, calls=%fused_computation.39 | convolution fusion | flops 4311744512 | bytes 17825792 | tf_op jit(solution)/shard_map/dot_general | solution.py:96
  72.0 0.3 copy.7
  72.3 0.7 reshape.100
  73.0 1.1 fusion.99
  74.1 1.3 fusion.38
  75.5 1.3 fusion.39
  76.8 1.3 convolution_add_fusion
  78.2 1.3 convolution_subtract_fusion
  79.5 2.7 copy.11
  82.2 3.5 stack.34
  85.7 2.7 copy.10
  88.5 3.5 stack.33
  92.0 1.5 maximum_multiply_fusion
  93.5 285.1 %reduce-scatter.2.cloned.1.call-done = f32[32,2,128]{2,0,1:T(8,128)} async-done(((f32[32,2,8192]{2,0,1:T(8,128)}), f32[32,2,128]{2,0,1:T(8,128)}) %reduce-scatter.2.cloned.1.call-update) | async-done | bytes 32784 | tf_op jit(solution)/shard_map/reduce_scatter | solution.py:107
  378.7 0.8 convert_element_type.37
  379.4 4.8 all_gather.6
  384.2 0.3 fusion.36
  384.6 0.6 pad_maximum_fusion.1
  385.2 106.7 %all-gather.2.cloned.1.call-done = bf16[32,2,8192]{2,0,1:T(8,128)(2,1)} async-done(((bf16[32,2,128]{2,0,1:T(8,128)(2,1)}), bf16[32,2,8192]{2,0,1:T(8,128)(2,1)}) %all-gather.2.cloned.1.call-update) | async-done | bytes 1048592 | tf_op jit(solution)/shard_map/all_gather | solution.py:111
  491.9 5.6 %reshape.101 = bf16[32,2,256,32]{3,2,0,1:T(8,128)(2,1)} reshape(bf16[32,2,8192]{2,0,1:T(8,128)(2,1)} %all-gather.2.cloned.1.call-done) | data formatting | bytes 2097152 | tf_op jit(solution)/shard_map/reshape | solution.py:112
  497.5 3.6 fusion.20
  501.1 3.4 fusion.21
  504.5 3.4 fusion.33
  508.0 1.9 fusion.32
  509.9 0.5 copy.14
  510.5 0.1 copy.47
  510.6 6.5 %convolution_multiply_fusion = f32[512,8192]{1,0:T(8,128)S(1)} fusion(bf16[512,512]{1,0:T(8,128)(2,1)S(1)} %bitcast.110, bf16[8192,256]{0,1:T(8,128)(2,1)} %get-tuple-element.12, bf16[8192,256]{0,1:T(8,128)(2,1)S(1)} %copy-done.1), kind=kOutput, calls=%fused_computation.12 | convolution fusion | flops 4315938816 | bytes 25690112 | tf_op jit(solution)/shard_map/dot_general | solution.py:116
  517.1 11.1 %fusion.7 = bf16[16,32,8192]{2,1,0:T(8,128)(2,1)} fusion(f32[16,32,8192]{2,1,0:T(8,128)S(1)} %bitcast.107, bf16[16,32,8192]{2,1,0:T(8,128)(2,1)} %param.4, f32[32]{0:T(128)S(1)} %copy-done.3, f32[32]{0:T(128)S(1)} %copy-done.4), kind=kLoop, calls=%fused_computation.8 | loop fusion | flops 54525952 | bytes 33554688 | tf_op jit(solution)/shard_map/convert_element_type | solution.py:129
  (24 shorter events, 0.3 us)
Async XLA Ops:
  6.5 372.1 %reduce-scatter.2.cloned.1.call-start = ((), (), s32[]{:S(2)}) async-start(), calls=%async_computation.1 | async-start | bytes 2129920 | tf_op jit(solution)/shard_map/reduce_scatter | solution.py:107
  85.7 298.5 %copy-start.2 = (bf16[2,64,32,128]{3,2,1,0:T(8,128)(2,1)S(1)}, bf16[2,64,32,128]{3,2,1,0:T(8,128)(2,1)}, u32[]{:S(2)}) copy-start(bf16[2,64,32,128]{3,2,1,0:T(8,128)(2,1)} %param.5) | copy-start | bytes 3145732
  93.5 398.4 %all-gather.2.cloned.1.call-start = ((), (), s32[]{:S(2)}) async-start(), calls=%async_computation.2 | async-start | bytes 1064960 | tf_op jit(solution)/shard_map/all_gather | solution.py:111
  497.5 10.5 %copy-start = (bf16[32,2,256,32]{3,2,0,1:T(8,128)(2,1)S(1)}, bf16[32,2,256,32]{3,2,0,1:T(8,128)(2,1)}, u32[]{:S(2)}) copy-start(bf16[32,2,256,32]{3,2,0,1:T(8,128)(2,1)} %reshape.101) | copy-start | bytes 3145732
  497.5 13.1 %copy-start.1 = (bf16[8192,256]{0,1:T(8,128)(2,1)S(1)}, bf16[8192,256]{0,1:T(8,128)(2,1)}, u32[]{:S(2)}) copy-start(bf16[8192,256]{0,1:T(8,128)(2,1)} %get-tuple-element.11) | copy-start | bytes 12582916
  510.6 6.5 %copy-start.3 = (f32[32]{0:T(128)S(1)}, f32[32]{0:T(128)}, u32[]{:S(2)}) copy-start(f32[32]{0:T(128)} %param.7) | copy-start | bytes 388
  510.6 6.5 %copy-start.4 = (f32[32]{0:T(128)S(1)}, f32[32]{0:T(128)}, u32[]{:S(2)}) copy-start(f32[32]{0:T(128)} %param.6) | copy-start | bytes 388
Sparse Core Ops, SparseCore 0:
  93.6 284.9 reduce-scatter.1
  385.3 106.5 all-gather.1
where the time goes:
time: 536 us; the launch traced here: 535 us
  waiting for transfers between devices  392 us (73%)
  other arithmetic  57.1 us (11%)
  local copies, waits for them, and re-layouts  35.6 us (7%)
  matrix products  32.1 us (6%)
  between operations  13.6 us (3%)
    reduce_scatter x1, waiting for transfers between devices, shards(): lax.psum_scatter(partial_modes, 'gx', scatter_dimension=2, tiled=True)  285 us
    all_gather x1, waiting for transfers between devices, shards(): whole_modes = lax.all_gather(mixed_local, 'gx', axis=2, tiled=True)  107 us
    another operation x1, other arithmetic  36.3 us
    add x1, local copies, waits for them, and re-layouts, yt_tables(): y_index[:, None, None, None] * y_freq[None, None, :, None] * TSTEPS  14.7 us
    convert_element_type x1, other arithmetic, shards(): return jax.nn.gelu(summed, approximate=True).astype(jnp.bfloat16)  11.1 us
  transfers between devices with their start and end apart: 2, of which 2 were waited for; matrix products, arithmetic and copies ran while one was open for 0% of the time, Pallas kernels for 0%

commit v1 on v0

v1 whole, which is shorter than its diff:
```python
import math

import jax
import jax.numpy as jnp
import ml_dtypes
import numpy as np
from jax import lax
from jax.experimental import pallas as pl
from jax.experimental.pallas import tpu as pltpu
from jax.sharding import PartitionSpec as P

MESH = pl.DeviceIdType.MESH
BF16 = jnp.bfloat16
F32 = jnp.float32

XCELLS = 1024
YCELLS = 128
TSTEPS = 64
KX = 32
KY = 32
KT = 8
PLANE = YCELLS * TSTEPS
FOLD = PLANE // 2
SLABS = 64
XDEV = 16
GROUP = 32
ROWS = XDEV * GROUP
HALF = ROWS // 2
PIECES = 4
PIECE = FOLD // PIECES
STEP = 512

NT = (((1,), (1,)), ((), ()))
TN = (((0,), (0,)), ((), ()))


def freq(index, number):
    return np.where(index < number // 2, index, index - number)


def plane_table():
    p, z, yh, xlo, half, r, kt4 = np.meshgrid(
        *[np.arange(n) for n in (2, 4, 2, 2, 2, 2, 4)], indexing="ij"
    )
    ky = freq((z * 8 + xlo * 4 + yh * 2 + p).reshape(-1), KY)
    kt = (half * 4 + kt4).reshape(-1)
    r = r.reshape(-1)
    cells = np.arange(FOLD)
    y, t = cells // TSTEPS, cells % TSTEPS
    phase = (ky[:, None] * y[None] * TSTEPS + kt[:, None] * t[None] * YCELLS) % PLANE
    angle = phase * (2.0 * math.pi / PLANE)
    table = np.where(r[:, None] == 0, np.cos(angle), -np.sin(angle))
    return table.astype(ml_dtypes.bfloat16)


def forward_x_table():
    kx = freq(np.arange(KX), KX)
    slot = np.arange(16)
    p, z, yh = slot // 8, (slot // 2) % 4, slot % 2
    angle = 2.0 * math.pi * ((kx[:, None] * (8 * z + yh * 2 + p)[None]) % 32) / 32
    cosine, sine = np.cos(angle), np.sin(angle)
    table = np.zeros((4, 2, 4, KX, 16, 4, 2, 4))
    for block in range(4):
        for k in range(4):
            table[block, 0, k, :, :, block, 0, k] = cosine
            table[block, 0, k, :, :, block, 1, k] = sine
            table[block, 1, k, :, :, block, 1, k] = cosine
            table[block, 1, k, :, :, block, 0, k] = -sine
    return table.reshape(1024, 512).astype(ml_dtypes.bfloat16)


def forward_twiddle():
    kx = freq(np.arange(KX), KX)
    scale = 1.0 / math.sqrt(XCELLS * PLANE)
    place = np.arange(4)
    offset = (place // 2) * 128 + (place % 2) * 16
    lanes = np.arange(ROWS) // GROUP
    angle = 2.0 * math.pi * ((kx[None, :, None] * (offset[:, None, None] + lanes)) % XCELLS) / XCELLS
    return (np.stack([np.cos(angle), np.sin(angle)], axis=1) * scale).astype(np.float32)


def inverse_x_table():
    kx = freq(np.arange(KX), KX)
    angle = 2.0 * math.pi * ((kx[None] * (8 * np.arange(128))[:, None]) % XCELLS) / XCELLS
    cosine, sine = np.cos(angle), np.sin(angle)
    table = np.zeros((128, 2, 4, 2, 4, KX))
    for k in range(4):
        table[:, 0, k, 0, k] = cosine
        table[:, 0, k, 1, k] = -sine
        table[:, 1, k, 0, k] = sine
        table[:, 1, k, 1, k] = cosine
    return table.reshape(1024, 256).astype(ml_dtypes.bfloat16)


def inverse_twiddle():
    kx = np.tile(freq(np.arange(KX), KX), 4)
    kt4 = np.repeat(np.arange(4), KX)
    lanes = np.arange(HALF) // GROUP
    angle = 2.0 * math.pi * ((kx[:, None] * lanes[None]) % XCELLS) / XCELLS
    parts = np.stack([np.cos(angle), np.sin(angle)])
    weight = np.stack([np.where(kt4 + 4 * half == 0, 1.0, 2.0) for half in range(2)])
    scale = 0.5 / math.sqrt(PLANE)
    return (parts[None] * weight[:, None, :, None] * scale).astype(np.float32)


def place_of(g):
    return g // 16, (g // 8) % 2, (g // 2) % 4, g % 2


def exchange_kernel(
    state, weight, table, fxt, ftw, ixt, itw, out,
    xbuf, tbuf, wbuf, fxt_v, ftw_v, ixt_v, itw_v,
    send1, recv1, partial, send2, recv2, modes, send3, recv3,
    tsem, xsem, csem, ssem, rsem,
):
    g = lax.axis_index("gx")
    col = lax.axis_index("col")
    z, xlo, y, core = place_of(g)

    def zy_partner(k):
        z2, y2 = (z + k // 4) % 4, (y + k % 4) % 4
        return z2 * 16 + xlo * 8 + y2 * 2 + core, (y2 % 2) * 8 + z2 * 2 + y2 // 2

    def near_partner(k):
        xlo2, core2, col2 = (xlo + (k // 2) % 2) % 2, (core + k % 2) % 2, (col + k // 4) % 2
        return z * 16 + xlo2 * 8 + y * 2 + core2, col2, xlo2 * 2 + core2

    loads = []
    for k in range(PIECES):
        cols = pl.ds(k * PIECE, PIECE)
        loads.append(pltpu.make_async_copy(table.at[:, cols], tbuf.at[:, cols], tsem.at[k]))
        loads[-1].start()
        for s in range(2):
            at = pl.ds(s * FOLD + k * PIECE, PIECE)
            pltpu.make_async_copy(
                state.at[pl.ds(0, HALF), at], xbuf.at[pl.ds(0, HALF), at], xsem.at[k * 2 + s]
            ).start()
    for k in range(PIECES):
        for s in range(2):
            at = pl.ds(s * FOLD + k * PIECE, PIECE)
            pltpu.make_async_copy(
                state.at[pl.ds(HALF, HALF), at],
                xbuf.at[pl.ds(HALF, HALF), at],
                xsem.at[2 * PIECES + k * 2 + s],
            ).start()
    constants = [
        pltpu.make_async_copy(fxt, fxt_v, csem.at[0]),
        pltpu.make_async_copy(ftw.at[xlo * 2 + core], ftw_v, csem.at[1]),
        pltpu.make_async_copy(weight, wbuf, csem.at[2]),
        pltpu.make_async_copy(itw.at[core], itw_v, csem.at[3]),
        pltpu.make_async_copy(ixt, ixt_v, csem.at[4]),
    ]
    for copy in constants:
        copy.start()

    barrier = pltpu.get_barrier_semaphore()

    @pl.loop(1, 64)
    def _(k):
        pl.semaphore_signal(barrier, inc=1, device_id=((g + k) % 64, col), device_id_type=MESH)

    @pl.loop(4, 8)
    def _(k):
        to, col2, _slot = near_partner(k)
        pl.semaphore_signal(barrier, inc=1, device_id=(to, col2), device_id_type=MESH)

    mine1 = (y % 2) * 8 + z * 2 + y // 2
    for h in range(2):
        rows = pl.ds(h * HALF, HALF)
        even = jnp.zeros((256, HALF), F32)
        odd = jnp.zeros((256, HALF), F32)
        for k in range(PIECES):
            lo = pl.ds(k * PIECE, PIECE)
            hi = pl.ds(FOLD + k * PIECE, PIECE)
            if h == 0:
                loads[k].wait()
            for s, at in ((0, lo), (1, hi)):
                pltpu.make_async_copy(
                    state.at[rows, at], xbuf.at[rows, at], xsem.at[h * 2 * PIECES + k * 2 + s]
                ).wait()
            x0, x1 = xbuf[rows, lo], xbuf[rows, hi]
            even += lax.dot_general(tbuf[0:256, lo], x0 + x1, NT, preferred_element_type=F32)
            odd += lax.dot_general(tbuf[256:512, lo], x0 - x1, NT, preferred_element_type=F32)
        send1[h, 0:8] = even.astype(BF16).reshape(8, 32, HALF)
        send1[h, 8:16] = odd.astype(BF16).reshape(8, 32, HALF)
        if h == 0:
            pl.semaphore_wait(barrier, 67)

        @pl.loop(1, 16)
        def _(k):
            to, slot = zy_partner(k)
            pltpu.make_async_remote_copy(
                send1.at[h, slot], recv1.at[h, mine1], ssem.at[h], rsem.at[h],
                device_id=(to, col), device_id_type=MESH,
            ).start()

        recv1[h, mine1] = send1[h, mine1]

    constants[0].wait()
    constants[1].wait()
    lane_c = lax.broadcasted_iota(jnp.int32, (GROUP, HALF), 1) % GROUP
    row_c = lax.broadcasted_iota(jnp.int32, (GROUP, HALF), 0)
    pick = jnp.where(lane_c == row_c, 1.0, 0.0).astype(BF16)
    for h in range(2):
        arrived = recv1.at[h, pl.ds(0, 15)]
        pltpu.make_async_copy(arrived, arrived, rsem.at[h]).wait()
        lanes = pl.ds(h * HALF, HALF)
        data = recv1[h].reshape(512, HALF)
        cosine, sine = ftw_v[0, :, lanes], ftw_v[1, :, lanes]
        for block in range(4):
            part = jnp.dot(fxt_v[pl.ds(block * 256, 256), :], data, preferred_element_type=F32)
            part = part.reshape(2, 4, KX, HALF)
            real, imag = part[0], part[1]
            turned = jnp.concatenate([
                real * cosine + imag * sine,
                imag * cosine - real * sine,
            ]).reshape(256, HALF).astype(BF16)
            summed = lax.dot_general(pick, turned, NT, preferred_element_type=F32)
            if h == 0:
                partial[block] = summed
            else:
                send2[block] = (partial[block] + summed).astype(BF16)

    mine2 = col * 4 + xlo * 2 + core

    @pl.loop(1, 8)
    def _(k):
        to, col2, block = near_partner(k)
        pltpu.make_async_remote_copy(
            send2.at[block], recv2.at[mine2], ssem.at[2], rsem.at[2],
            device_id=(to, col2), device_id_type=MESH,
        ).start()

    recv2[mine2] = send2[xlo * 2 + core]
    for copy in constants[2:]:
        copy.wait()
    arrived = recv2.at[pl.ds(0, 7)]
    pltpu.make_async_copy(arrived, arrived, rsem.at[2]).wait()
    for c in range(2):
        total = recv2[c * 4].astype(F32)
        for k in range(1, 4):
            total += recv2[c * 4 + k].astype(F32)
        total = total.astype(BF16).astype(F32)
        modes[0, pl.ds(c * GROUP, GROUP), :] = total[:, 0:128]
        modes[1, pl.ds(c * GROUP, GROUP), :] = total[:, 128:256]

    def mix(step, sums):
        real, imag = sums
        rows = pl.ds(pl.multiple_of(step * 8, 8), 8)
        mrs, mis = modes[0, rows, :], modes[1, rows, :]
        for k in range(8):
            mr, mi = mrs[k:k + 1], mis[k:k + 1]
            wr, wi = wbuf[0, step * 8 + k].astype(F32), wbuf[1, step * 8 + k].astype(F32)
            real, imag = real + (wr * mr - wi * mi), imag + (wr * mi + wi * mr)
        return real, imag

    zero = jnp.zeros((GROUP, 128), F32)
    real, imag = lax.fori_loop(0, 8, mix, (zero, zero))
    mixed = jnp.concatenate([real, imag], axis=1).astype(BF16)
    spread = lax.dot_general(mixed, pick, TN, preferred_element_type=F32)
    cosine, sine = itw_v[0], itw_v[1]
    real, imag = spread[0:128], spread[128:256]
    turned = jnp.concatenate([
        real * cosine - imag * sine,
        real * sine + imag * cosine,
    ]).astype(BF16)
    for q in range(4):
        rows = jnp.dot(ixt_v[pl.ds(q * 256, 256), :], turned, preferred_element_type=F32)
        send3[pl.ds(q * 16, 16)] = rows.astype(BF16).reshape(16, 16, HALF)

    mine3 = (y % 2) * 32 + (z * 2 + y // 2) * 4 + xlo * 2 + core

    @pl.loop(1, 64)
    def _(k):
        to = (g + k) % 64
        pltpu.make_async_remote_copy(
            send3.at[to], recv3.at[mine3], ssem.at[3], rsem.at[3],
            device_id=(to, col), device_id_type=MESH,
        ).start()

    recv3[mine3] = send3[g]
    arrived = recv3.at[pl.ds(0, 63)]
    pltpu.make_async_copy(arrived, arrived, rsem.at[3]).wait()
    out[...] = recv3[...]
    for h in range(2):
        sent = send1.at[h, pl.ds(0, 15)]
        pltpu.make_async_copy(sent, sent, ssem.at[h]).wait()
    sent = recv2.at[pl.ds(0, 7)]
    pltpu.make_async_copy(sent, sent, ssem.at[2]).wait()
    sent = send3.at[pl.ds(0, 63)]
    pltpu.make_async_copy(sent, sent, ssem.at[3]).wait()


def finish_kernel(slabs, table, state, gain, bias, out, vals, tbuf, xbuf, obuf, tsem, xsem, osem):
    steps = FOLD // STEP

    def load(j):
        at = pl.ds(j * STEP, STEP)
        slot = j % 2
        copies = [pltpu.make_async_copy(table.at[:, at], tbuf.at[slot], tsem.at[slot])]
        for s in range(2):
            at = pl.ds(s * FOLD + j * STEP, STEP)
            copies.append(pltpu.make_async_copy(state.at[:, at], xbuf.at[slot, s], xsem.at[slot, s]))
        return copies

    def store(j):
        slot = j % 2
        return [
            pltpu.make_async_copy(
                obuf.at[slot, s], out.at[:, pl.ds(s * FOLD + j * STEP, STEP)], osem.at[slot, s]
            )
            for s in range(2)
        ]

    for copy in load(0):
        copy.start()
    for h in range(2):
        part = slabs[...].astype(F32)[:, h * 8:(h + 1) * 8, :].reshape(512, HALF)
        vals[pl.ds(h * HALF, HALF), :] = part.T.astype(BF16)
    square = (GROUP, GROUP)
    diagonal = lax.broadcasted_iota(jnp.int32, square, 0) == lax.broadcasted_iota(jnp.int32, square, 1)
    gain_c = 0.5 * jnp.sum(jnp.where(diagonal, gain[...], 0.0), axis=1, keepdims=True)
    bias_c = 0.5 * jnp.sum(jnp.where(diagonal, bias[...], 0.0), axis=1, keepdims=True)
    c1 = 2.0 * math.sqrt(2.0 / math.pi)
    c3 = 8.0 * 0.044715 * math.sqrt(2.0 / math.pi)
    for j in range(steps):
        slot = j % 2
        if j + 1 < steps:
            for copy in load(j + 1):
                copy.start()
        for copy in load(j):
            copy.wait()
        if j >= 2:
            for copy in store(j - 2):
                copy.wait()

        @pl.loop(0, ROWS // 128)
        def _(m):
            rows = pl.ds(pl.multiple_of(m * 128, 128), 128)
            even = jnp.dot(vals[rows, 0:256], tbuf[slot, 0:256, :], preferred_element_type=F32)
            odd = jnp.dot(vals[rows, 256:512], tbuf[slot, 256:512, :], preferred_element_type=F32)
            for s in range(2):
                spectral = even + odd if s == 0 else even - odd
                local = xbuf[slot, s, rows, :].astype(F32).reshape(4, GROUP, STEP)
                v = spectral.reshape(4, GROUP, STEP) + (local * gain_c + bias_c)
                u = v * (c1 + c3 * (v * v))
                res = v + v * jnp.tanh(u)
                obuf[slot, s, rows, :] = res.reshape(128, STEP).astype(BF16)

        for copy in store(j):
            copy.start()
    for j in (steps - 2, steps - 1):
        for copy in store(j):
            copy.wait()


def shards(state_field, spectral_weight, local_weight, channel_bias):
    state = state_field.reshape(ROWS, PLANE)
    table = jnp.asarray(plane_table())
    anywhere = pl.BlockSpec(memory_space=pl.ANY)
    vmem = pl.BlockSpec(memory_space=pltpu.VMEM)
    slabs = pl.pallas_call(
        exchange_kernel,
        out_shape=jax.ShapeDtypeStruct((64, 16, HALF), BF16),
        in_specs=[anywhere] * 7,
        out_specs=vmem,
        scratch_shapes=[
            pltpu.VMEM((ROWS, PLANE), BF16),
            pltpu.VMEM((512, FOLD), BF16),
            pltpu.VMEM((2, 64, GROUP, 128), BF16),
            pltpu.VMEM((1024, 512), BF16),
            pltpu.VMEM((2, KX, ROWS), F32),
            pltpu.VMEM((1024, 256), BF16),
            pltpu.VMEM((2, 128, HALF), F32),
            pltpu.VMEM((2, 16, 32, HALF), BF16),
            pltpu.VMEM((2, 16, 32, HALF), BF16),
            pltpu.VMEM((4, GROUP, 256), F32),
            pltpu.VMEM((4, GROUP, 256), BF16),
            pltpu.VMEM((8, GROUP, 256), BF16),
            pltpu.VMEM((2, 64, 128), F32),
            pltpu.VMEM((64, 16, HALF), BF16),
            pltpu.VMEM((64, 16, HALF), BF16),
            pltpu.SemaphoreType.DMA((PIECES,)),
            pltpu.SemaphoreType.DMA((4 * PIECES,)),
            pltpu.SemaphoreType.DMA((5,)),
            pltpu.SemaphoreType.DMA((4,)),
            pltpu.SemaphoreType.DMA((4,)),
        ],
        compiler_params=pltpu.CompilerParams(
            collective_id=0, has_side_effects=True, vmem_limit_bytes=48 << 20
        ),
        name="exchange",
    )(
        state,
        spectral_weight,
        table,
        jnp.asarray(forward_x_table()),
        jnp.asarray(forward_twiddle()),
        jnp.asarray(inverse_x_table()),
        jnp.asarray(inverse_twiddle()),
    )
    result = pl.pallas_call(
        finish_kernel,
        out_shape=jax.ShapeDtypeStruct((ROWS, PLANE), BF16),
        in_specs=[vmem, anywhere, anywhere, vmem, vmem],
        out_specs=anywhere,
        scratch_shapes=[
            pltpu.VMEM((ROWS, 512), BF16),
            pltpu.VMEM((2, 512, STEP), BF16),
            pltpu.VMEM((2, 2, ROWS, STEP), BF16),
            pltpu.VMEM((2, 2, ROWS, STEP), BF16),
            pltpu.SemaphoreType.DMA((2,)),
            pltpu.SemaphoreType.DMA((2, 2)),
            pltpu.SemaphoreType.DMA((2, 2)),
        ],
        compiler_params=pltpu.CompilerParams(vmem_limit_bytes=32 << 20),
        name="finish",
    )(slabs, table, state, local_weight.reshape(1, GROUP), channel_bias.reshape(1, GROUP))
    return result.reshape(state_field.shape)


def solution(mesh):
    return jax.shard_map(
        shards,
        mesh=mesh,
        in_specs=(P("gx", "col", None), P(None, None, "col", "gx"), P("col"), P("col")),
        out_specs=P("gx", "col", None),
        check_vma=False,
    )
```

time: 536 us -> 60.2 us (0.11)
  waiting for transfers between devices: 392 us -> 0 us
  other arithmetic: 57.1 us -> 0 us
  Pallas kernels: 0 us -> 52 us
  matrix products: 32.1 us -> 0 us
  local copies, waits for them, and re-layouts: 35.6 us -> 7.77 us
  between operations: 13.6 us -> 0.05 us
    reduce_scatter x1 -> x0, waiting for transfers between devices: 285 us -> none  [shards(): lax.psum_scatter(partial_modes, 'gx', scatter_dimension=2, tiled=True)]
    all_gather x1 -> x0, waiting for transfers between devices: 107 us -> none  [shards(): whole_modes = lax.all_gather(mixed_local, 'gx', axis=2, tiled=True)]
    pallas_call x0 -> x2, Pallas kernels: none -> 52 us  [the longest x1 35.2 us: shards(): pl.pallas_call(exchange_kernel, out_shape=jax.ShapeDtypeStruct((64, 16, H...]
    another operation x4 -> x0, other arithmetic: 37 us -> none
    dot_general x10 -> x0, matrix products: 32.1 us -> none  [the longest x1 7.9 us: shards(): jnp.dot(state_field.reshape(slab_rows * group_size, plane_cells), forward...]
    add x2 -> x0, local copies, waits for them, and re-layouts: 17.4 us -> none  [the longest x1 14.7 us: yt_tables(): y_index[:, None, None, None] * y_freq[None, None, :, None] * TSTEPS]
    convert_element_type x2 -> x0, other arithmetic: 11.9 us -> none  [the longest x1 11.1 us: shards(): return jax.nn.gelu(summed, approximate=True).astype(jnp.bfloat16)]
    unnamed x11 -> x18, local copies, waits for them, and re-layouts: 0.11 us -> 7.77 us
  transfers between devices with their start and end apart: 2 -> 0, of which waited for: 2 -> 0; matrix products, arithmetic and copies ran while one was open for 0% -> 0% of each run, Pallas kernels for 0% -> 0%
where the time goes in v1:
time: 60.2 us; the launch traced here: 59.9 us
  Pallas kernels  52 us (86%)
  local copies, waits for them, and re-layouts  7.77 us (13%)
    pallas_call x1, Pallas kernels, shards(): pl.pallas_call(exchange_kernel, out_shape=jax.ShapeDtypeStruct((64, 16, H...  35.2 us
    pallas_call x1, Pallas kernels, shards(): pl.pallas_call(finish_kernel, out_shape=jax.ShapeDtypeStruct((ROWS, PLANE...  16.9 us
    unnamed x18, local copies, waits for them, and re-layouts  7.77 us

profile of v1, /device:TPU:1, one launch (start us, length us, event | category | flops | bytes accessed | tf_op | source)
XLA Modules:
  0.0 59.9 jit_solution(10063893222184262078)
XLA Ops:
  0.0 0.0 copy-start.2
  0.0 1.2 %copy-done.2 = bf16[2,64,32,128]{3,2,1,0:T(8,128)(2,1)S(1)} copy-done((bf16[2,64,32,128]{3,2,1,0:T(8,128)(2,1)S(1)}, bf16[2,64,32,128]{3,2,1,0:T(8,128)(2,1)}, u32[]{:S(2)}) %copy-start.2) | copy-done | bytes 1048600
  1.2 0.0 copy-start.3
  1.2 1.2 %copy-done.3 = bf16[1024,512]{1,0:T(8,128)(2,1)S(1)} copy-done((bf16[1024,512]{1,0:T(8,128)(2,1)S(1)}, bf16[1024,512]{1,0:T(8,128)(2,1)}, u32[]{:S(2)}) %copy-start.3) | copy-done | bytes 1048600
  2.5 0.0 copy-start.4
  2.5 1.0 %copy-done.4 = f32[2,2,128,256]{3,2,1,0:T(8,128)S(1)} copy-done((f32[2,2,128,256]{3,2,1,0:T(8,128)S(1)}, f32[2,2,128,256]{3,2,1,0:T(8,128)}, u32[]{:S(2)}) %copy-start.4) | copy-done | bytes 524312
  3.5 0.0 copy-start.5
  3.5 1.0 %copy-done.5 = bf16[1024,256]{1,0:T(8,128)(2,1)S(1)} copy-done((bf16[1024,256]{1,0:T(8,128)(2,1)S(1)}, bf16[1024,256]{1,0:T(8,128)(2,1)}, u32[]{:S(2)}) %copy-start.5) | copy-done | bytes 524312
  4.5 0.0 copy-start.6
  4.5 1.0 %copy-done.6 = f32[4,2,32,512]{3,2,1,0:T(8,128)S(1)} copy-done((f32[4,2,32,512]{3,2,1,0:T(8,128)S(1)}, f32[4,2,32,512]{3,2,1,0:T(8,128)}, u32[]{:S(2)}) %copy-start.6) | copy-done | bytes 524312
  5.6 0.0 copy-start
  5.6 0.0 copy-start.7
  5.6 0.0 copy-start.8
  5.6 35.2 %exchange.1.slabs = bf16[64,16,256]{2,1,0:T(8,128)(2,1)S(1)} custom-call(bf16[512,8192]{1,0:T(8,128)(2,1)} %bitcast.4, bf16[2,64,32,128]{3,2,1,0:T(8,128)(2,1)S(1)} %copy-done.2, bf16[512,4096]{1,0:T(8,128)(2,1)} %constant.10.clone.table, bf16[1024,512]{1,0:T(8,128)(2,1)S(1)} %copy-done.3, f32[4,2,32,512]{3,2,1,0:T(8,128)S(1)} %copy-done.6, ...), custom_call_target="tpu_custom_call" | custom-call | tf_op jit(solution)/shard_map/exchange/pallas_call | solution.py:362
  40.7 0.0 copy-done
  40.8 0.0 copy-done.7
  40.8 0.0 copy-done.8
  40.8 0.0 copy-start.1
  40.8 2.2 %copy-done.1 = bf16[512,4096]{1,0:T(8,128)(2,1)S(1)} copy-done((bf16[512,4096]{1,0:T(8,128)(2,1)S(1)}, bf16[512,4096]{1,0:T(8,128)(2,1)}, u32[]{:S(2)}) %copy-start.1) | copy-done | bytes 4194328
  43.0 16.9 %finish.1 = bf16[512,8192]{1,0:T(8,128)(2,1)} custom-call(bf16[64,16,256]{2,1,0:T(8,128)(2,1)S(1)} %exchange.1.slabs, bf16[512,4096]{1,0:T(8,128)(2,1)S(1)} %copy-done.1, bf16[512,8192]{1,0:T(8,128)(2,1)S(1)} %bitcast.5, f32[1,32]{1,0:T(1,128)S(1)} %bitcast.6, f32[1,32]{1,0:T(1,128)S(1)} %bitcast.7), custom_call_target="tpu_custom_call" | custom-call | tf_op jit(solution)/shard_map/finish/pallas_call | solution.py:402
Async XLA Ops:
  0.0 1.2 %copy-start.2 = (bf16[2,64,32,128]{3,2,1,0:T(8,128)(2,1)S(1)}, bf16[2,64,32,128]{3,2,1,0:T(8,128)(2,1)}, u32[]{:S(2)}) copy-start(bf16[2,64,32,128]{3,2,1,0:T(8,128)(2,1)} %weight.1) | copy-start | bytes 3145732
  1.2 1.2 %copy-start.3 = (bf16[1024,512]{1,0:T(8,128)(2,1)S(1)}, bf16[1024,512]{1,0:T(8,128)(2,1)}, u32[]{:S(2)}) copy-start(bf16[1024,512]{1,0:T(8,128)(2,1)} %constant.11.clone.fxt) | copy-start | bytes 3145732
  2.5 1.0 %copy-start.4 = (f32[2,2,128,256]{3,2,1,0:T(8,128)S(1)}, f32[2,2,128,256]{3,2,1,0:T(8,128)}, u32[]{:S(2)}) copy-start(f32[2,2,128,256]{3,2,1,0:T(8,128)} %constant.14.clone.itw) | copy-start | bytes 1572868
  3.5 1.0 %copy-start.5 = (bf16[1024,256]{1,0:T(8,128)(2,1)S(1)}, bf16[1024,256]{1,0:T(8,128)(2,1)}, u32[]{:S(2)}) copy-start(bf16[1024,256]{1,0:T(8,128)(2,1)} %constant.13.clone.ixt) | copy-start | bytes 1572868
  4.5 1.0 %copy-start.6 = (f32[4,2,32,512]{3,2,1,0:T(8,128)S(1)}, f32[4,2,32,512]{3,2,1,0:T(8,128)}, u32[]{:S(2)}) copy-start(f32[4,2,32,512]{3,2,1,0:T(8,128)} %constant.12.clone.ftw) | copy-start | bytes 1572868
  5.6 35.2 %copy-start = (bf16[16,32,8192]{2,1,0:T(8,128)(2,1)S(1)}, bf16[16,32,8192]{2,1,0:T(8,128)(2,1)}, u32[]{:S(2)}) copy-start(bf16[16,32,8192]{2,1,0:T(8,128)(2,1)} %param.9) | copy-start | bytes 25165828
  5.6 35.2 %copy-start.7 = (f32[32]{0:T(128)S(1)}, f32[32]{0:T(128)}, u32[]{:S(2)}) copy-start(f32[32]{0:T(128)} %param.11) | copy-start | bytes 388
  5.6 35.2 %copy-start.8 = (f32[32]{0:T(128)S(1)}, f32[32]{0:T(128)}, u32[]{:S(2)}) copy-start(f32[32]{0:T(128)} %param.12) | copy-start | bytes 388
  40.8 2.2 %copy-start.1 = (bf16[512,4096]{1,0:T(8,128)(2,1)S(1)}, bf16[512,4096]{1,0:T(8,128)(2,1)}, u32[]{:S(2)}) copy-start(bf16[512,4096]{1,0:T(8,128)(2,1)} %constant.10.clone.table) | copy-start | bytes 12582916

commit v2 on v1

--- a/solution.py
+++ b/solution.py
@@ -29,6 +29,9 @@
 PIECES = 4
 PIECE = FOLD // PIECES
 STEP = 512
+BLOCK = 256
+MB = 64
+PRE = 256
 
 NT = (((1,), (1,)), ((), ()))
 TN = (((0,), (0,)), ((), ()))
@@ -108,8 +111,8 @@
 
 
 def exchange_kernel(
-    state, weight, table, fxt, ftw, ixt, itw, out,
-    xbuf, tbuf, wbuf, fxt_v, ftw_v, ixt_v, itw_v,
+    state, weight, gain, bias, table, fxt, ftw, ixt, itw, out, pre, tbuf,
+    xbuf, wbuf, gain_v, bias_v, fxt_v, ftw_v, ixt_v, itw_v,
     send1, recv1, partial, send2, recv2, modes, send3, recv3,
     tsem, xsem, csem, ssem, rsem,
 ):
@@ -150,8 +153,20 @@
         pltpu.make_async_copy(itw.at[core], itw_v, csem.at[3]),
         pltpu.make_async_copy(ixt, ixt_v, csem.at[4]),
     ]
-    for copy in constants:
+    local_copies = [
+        pltpu.make_async_copy(gain, gain_v, csem.at[5]),
+        pltpu.make_async_copy(bias, bias_v, csem.at[6]),
+    ]
+    for copy in constants + local_copies:
         copy.start()
+
+    square = (GROUP, GROUP)
+    diagonal = lax.broadcasted_iota(jnp.int32, square, 0) == lax.broadcasted_iota(jnp.int32, square, 1)
+
+    def column(row):
+        part = 0.5 * jnp.sum(jnp.where(diagonal, row, 0.0), axis=1, keepdims=True)
+        return jnp.broadcast_to(part, (GROUP, PRE))
+
 
     barrier = pltpu.get_barrier_semaphore()
 
@@ -195,6 +210,16 @@
             ).start()
 
         recv1[h, mine1] = send1[h, mine1]
+
+    local_copies[0].wait()
+    local_copies[1].wait()
+    gain_c, bias_c = column(gain_v[...]), column(bias_v[...])
+
+    @pl.loop(0, XDEV)
+    def _(x):
+        rows = pl.ds(pl.multiple_of(x * GROUP, GROUP), GROUP)
+        for at in range(0, PLANE, PRE):
+            pre[rows, pl.ds(at, PRE)] = xbuf[rows, pl.ds(at, PRE)].astype(F32) * gain_c + bias_c
 
     constants[0].wait()
     constants[1].wait()
@@ -291,62 +316,44 @@
     pltpu.make_async_copy(sent, sent, ssem.at[3]).wait()
 
 
-def finish_kernel(slabs, table, state, gain, bias, out, vals, tbuf, xbuf, obuf, tsem, xsem, osem):
-    steps = FOLD // STEP
-
-    def load(j):
-        at = pl.ds(j * STEP, STEP)
-        slot = j % 2
-        copies = [pltpu.make_async_copy(table.at[:, at], tbuf.at[slot], tsem.at[slot])]
-        for s in range(2):
-            at = pl.ds(s * FOLD + j * STEP, STEP)
-            copies.append(pltpu.make_async_copy(state.at[:, at], xbuf.at[slot, s], xsem.at[slot, s]))
-        return copies
+def finish_kernel(slabs, pre, table, out, vals, obuf, evens, odds, osem):
+    c1 = 2.0 * math.sqrt(2.0 / math.pi)
+    c3 = 8.0 * 0.044715 * math.sqrt(2.0 / math.pi)
 
     def store(j):
-        slot = j % 2
         return [
             pltpu.make_async_copy(
-                obuf.at[slot, s], out.at[:, pl.ds(s * FOLD + j * STEP, STEP)], osem.at[slot, s]
+                obuf.at[j % 2, s], out.at[:, pl.ds(s * FOLD + j * STEP, STEP)], osem.at[j % 2, s]
             )
             for s in range(2)
         ]
 
-    for copy in load(0):
-        copy.start()
+    def products(n):
+        cols = pl.ds(n * BLOCK, BLOCK)
+        evens[n % 2] = jnp.dot(vals[:, 0:256], table[0:256, cols], preferred_element_type=F32)
+        odds[n % 2] = jnp.dot(vals[:, 256:512], table[256:512, cols], preferred_element_type=F32)
+
     for h in range(2):
         part = slabs[...].astype(F32)[:, h * 8:(h + 1) * 8, :].reshape(512, HALF)
         vals[pl.ds(h * HALF, HALF), :] = part.T.astype(BF16)
-    square = (GROUP, GROUP)
-    diagonal = lax.broadcasted_iota(jnp.int32, square, 0) == lax.broadcasted_iota(jnp.int32, square, 1)
-    gain_c = 0.5 * jnp.sum(jnp.where(diagonal, gain[...], 0.0), axis=1, keepdims=True)
-    bias_c = 0.5 * jnp.sum(jnp.where(diagonal, bias[...], 0.0), axis=1, keepdims=True)
-    c1 = 2.0 * math.sqrt(2.0 / math.pi)
-    c3 = 8.0 * 0.044715 * math.sqrt(2.0 / math.pi)
+    products(0)
+    steps = FOLD // STEP
     for j in range(steps):
-        slot = j % 2
-        if j + 1 < steps:
-            for copy in load(j + 1):
-                copy.start()
-        for copy in load(j):
-            copy.wait()
         if j >= 2:
             for copy in store(j - 2):
                 copy.wait()
-
-        @pl.loop(0, ROWS // 128)
-        def _(m):
-            rows = pl.ds(pl.multiple_of(m * 128, 128), 128)
-            even = jnp.dot(vals[rows, 0:256], tbuf[slot, 0:256, :], preferred_element_type=F32)
-            odd = jnp.dot(vals[rows, 256:512], tbuf[slot, 256:512, :], preferred_element_type=F32)
-            for s in range(2):
-                spectral = even + odd if s == 0 else even - odd
-                local = xbuf[slot, s, rows, :].astype(F32).reshape(4, GROUP, STEP)
-                v = spectral.reshape(4, GROUP, STEP) + (local * gain_c + bias_c)
-                u = v * (c1 + c3 * (v * v))
-                res = v + v * jnp.tanh(u)
-                obuf[slot, s, rows, :] = res.reshape(128, STEP).astype(BF16)
-
+        for i in range(STEP // BLOCK):
+            n = j * (STEP // BLOCK) + i
+            if (n + 1) * BLOCK < FOLD:
+                products(n + 1)
+            for m in range(ROWS // MB):
+                rows = pl.ds(m * MB, MB)
+                even, odd = evens[n % 2, rows, :], odds[n % 2, rows, :]
+                for s in range(2):
+                    spectral = even + odd if s == 0 else even - odd
+                    v = spectral + pre[rows, pl.ds(s * FOLD + n * BLOCK, BLOCK)]
+                    u = v * (c1 + c3 * (v * v))
+                    obuf[j % 2, s, rows, pl.ds(i * BLOCK, BLOCK)] = (v + v * jnp.tanh(u)).astype(BF16)
         for copy in store(j):
             copy.start()
     for j in (steps - 2, steps - 1):
@@ -354,20 +361,28 @@
             copy.wait()
 
 
+def in_hbm(array):
+    return pltpu.with_memory_space_constraint(array, pltpu.HBM)
+
+
 def shards(state_field, spectral_weight, local_weight, channel_bias):
     state = state_field.reshape(ROWS, PLANE)
-    table = jnp.asarray(plane_table())
-    anywhere = pl.BlockSpec(memory_space=pl.ANY)
+    anywhere = pl.BlockSpec(memory_space=pltpu.HBM)
     vmem = pl.BlockSpec(memory_space=pltpu.VMEM)
-    slabs = pl.pallas_call(
+    slabs, pre, table_v = pl.pallas_call(
         exchange_kernel,
-        out_shape=jax.ShapeDtypeStruct((64, 16, HALF), BF16),
-        in_specs=[anywhere] * 7,
-        out_specs=vmem,
+        out_shape=[
+            jax.ShapeDtypeStruct((64, 16, HALF), BF16),
+            jax.ShapeDtypeStruct((ROWS, PLANE), F32),
+            jax.ShapeDtypeStruct((512, FOLD), BF16),
+        ],
+        in_specs=[anywhere] * 9,
+        out_specs=[vmem] * 3,
         scratch_shapes=[
             pltpu.VMEM((ROWS, PLANE), BF16),
-            pltpu.VMEM((512, FOLD), BF16),
             pltpu.VMEM((2, 64, GROUP, 128), BF16),
+            pltpu.VMEM((1, GROUP), F32),
+            pltpu.VMEM((1, GROUP), F32),
             pltpu.VMEM((1024, 512), BF16),
             pltpu.VMEM((2, KX, ROWS), F32),
             pltpu.VMEM((1024, 256), BF16),
@@ -382,40 +397,38 @@
             pltpu.VMEM((64, 16, HALF), BF16),
             pltpu.SemaphoreType.DMA((PIECES,)),
             pltpu.SemaphoreType.DMA((4 * PIECES,)),
-            pltpu.SemaphoreType.DMA((5,)),
+            pltpu.SemaphoreType.DMA((7,)),
             pltpu.SemaphoreType.DMA((4,)),
             pltpu.SemaphoreType.DMA((4,)),
         ],
         compiler_params=pltpu.CompilerParams(
-            collective_id=0, has_side_effects=True, vmem_limit_bytes=48 << 20
+            collective_id=0, has_side_effects=True, vmem_limit_bytes=20 << 20
         ),
         name="exchange",
     )(
-        state,
-        spectral_weight,
-        table,
-        jnp.asarray(forward_x_table()),
-        jnp.asarray(forward_twiddle()),
-        jnp.asarray(inverse_x_table()),
-        jnp.asarray(inverse_twiddle()),
+        in_hbm(state),
+        in_hbm(spectral_weight),
+        in_hbm(local_weight.reshape(1, GROUP)),
+        in_hbm(channel_bias.reshape(1, GROUP)),
+        *[in_hbm(jnp.asarray(table())) for table in (
+            plane_table, forward_x_table, forward_twiddle, inverse_x_table, inverse_twiddle
+        )],
     )
     result = pl.pallas_call(
         finish_kernel,
         out_shape=jax.ShapeDtypeStruct((ROWS, PLANE), BF16),
-        in_specs=[vmem, anywhere, anywhere, vmem, vmem],
+        in_specs=[vmem] * 3,
         out_specs=anywhere,
         scratch_shapes=[
             pltpu.VMEM((ROWS, 512), BF16),
-            pltpu.VMEM((2, 512, STEP), BF16),
             pltpu.VMEM((2, 2, ROWS, STEP), BF16),
-            pltpu.VMEM((2, 2, ROWS, STEP), BF16),
-            pltpu.SemaphoreType.DMA((2,)),
-            pltpu.SemaphoreType.DMA((2, 2)),
+            pltpu.VMEM((2, ROWS, BLOCK), F32),
+            pltpu.VMEM((2, ROWS, BLOCK), F32),
             pltpu.SemaphoreType.DMA((2, 2)),
         ],
-        compiler_params=pltpu.CompilerParams(vmem_limit_bytes=32 << 20),
+        compiler_params=pltpu.CompilerParams(vmem_limit_bytes=16 << 20),
         name="finish",
-    )(slabs, table, state, local_weight.reshape(1, GROUP), channel_bias.reshape(1, GROUP))
+    )(slabs, pre, table_v)
     return result.reshape(state_field.shape)
 
 

time: 60.2 us -> 44.1 us (0.73)
  Pallas kernels: 52 us -> 44 us
  local copies, waits for them, and re-layouts: 7.77 us -> 0 us
    pallas_call x1, Pallas kernels: 16.9 us -> 8.22 us  [shards(): pl.pallas_call(finish_kernel, out_shape=jax.ShapeDtypeStruct((ROWS, PLANE...]
    unnamed x18 -> x0, local copies, waits for them, and re-layouts: 7.77 us -> none
    pallas_call x1, Pallas kernels: 35.2 us -> 35.8 us  [shards(): pl.pallas_call(exchange_kernel, out_shape=[jax.ShapeDtypeStruct((64, 16,...]
where the time goes in v2:
time: 44.1 us; the launch traced here: 44 us
  Pallas kernels  44 us (100%)
    pallas_call x1, Pallas kernels, shards(): pl.pallas_call(exchange_kernel, out_shape=[jax.ShapeDtypeStruct((64, 16,...  35.8 us
    pallas_call x1, Pallas kernels, shards(): pl.pallas_call(finish_kernel, out_shape=jax.ShapeDtypeStruct((ROWS, PLANE...  8.22 us

profile of v2, /device:TPU:1, one launch (start us, length us, event | category | flops | bytes accessed | tf_op | source)
XLA Modules:
  0.0 44.0 jit_solution(15804023783683073536)
XLA Ops:
  0.0 35.8 %exchange.1 = (bf16[64,16,256]{2,1,0:T(8,128)(2,1)S(1)}, f32[512,8192]{1,0:T(8,128)S(1)}, bf16[512,4096]{1,0:T(8,128)(2,1)S(1)}) custom-call(bf16[512,8192]{1,0:T(8,128)(2,1)} %bitcast.4, bf16[2,64,32,128]{3,2,1,0:T(8,128)(2,1)} %weight.1, f32[1,32]{1,0:T(1,128)} %bitcast.5, f32[1,32]{1,0:T(1,128)} %bitcast.6, bf16[512,4096]{1,0:T(8,128)(2,1)} %constant.10.clone.table, ...), custom_call_target="tpu_custom_call" | custom-call | tf_op jit(solution)/shard_map/exchange/pallas_call | solution.py:372
  35.8 8.2 %finish.1 = bf16[512,8192]{1,0:T(8,128)(2,1)} custom-call(bf16[64,16,256]{2,1,0:T(8,128)(2,1)S(1)} %get-tuple-element.8.slabs, f32[512,8192]{1,0:T(8,128)S(1)} %get-tuple-element.9.pre, bf16[512,4096]{1,0:T(8,128)(2,1)S(1)} %get-tuple-element.10.table), custom_call_target="tpu_custom_call" | custom-call | tf_op jit(solution)/shard_map/finish/pallas_call | solution.py:417

commit v3 on v2

v3 whole, which is shorter than its diff:
```python
import math

import jax
import jax.numpy as jnp
import ml_dtypes
import numpy as np
from jax import lax
from jax.experimental import pallas as pl
from jax.experimental.pallas import tpu as pltpu
from jax.sharding import PartitionSpec as P

MESH = pl.DeviceIdType.MESH
BF16 = jnp.bfloat16
F32 = jnp.float32

XCELLS = 1024
YCELLS = 128
TSTEPS = 64
KX = 32
KY = 32
PLANE = YCELLS * TSTEPS
FOLD = PLANE // 2
QUARTER = PLANE // 4
XDEV = 16
GROUP = 32
ROWS = XDEV * GROUP
HALF = ROWS // 2
PIECES = 4
PIECE = FOLD // PIECES
STEP = 512
BLOCK = 256
MB = 64
PRE = 256

NT = (((1,), (1,)), ((), ()))
TN = (((0,), (0,)), ((), ()))


FAR_FIRST = sorted(
    [(dz, dy) for dz in range(4) for dy in range(4) if dz or dy],
    key=lambda o: -(min(o[0], 4 - o[0]) + min(o[1], 4 - o[1])),
)


def freq(index, number):
    return np.where(index < number // 2, index, index - number)


def plane_table():
    p, c, z, yh, xlo, half, r, kt2 = np.meshgrid(
        *[np.arange(n) for n in (2, 2, 4, 2, 2, 2, 2, 2)], indexing="ij"
    )
    ky = freq((z * 8 + xlo * 4 + yh * 2 + p).reshape(-1), KY)
    kt = (half * 4 + c * 2 + kt2).reshape(-1)
    r = r.reshape(-1)
    cells = np.arange(FOLD)
    y, t = cells // TSTEPS, cells % TSTEPS
    phase = (ky[:, None] * y[None] * TSTEPS + kt[:, None] * t[None] * YCELLS) % PLANE
    angle = phase * (2.0 * math.pi / PLANE)
    table = np.where(r[:, None] == 0, np.cos(angle), -np.sin(angle))
    return table.astype(ml_dtypes.bfloat16)


def forward_x_table():
    kx = freq(np.arange(KX), KX)
    slot = np.arange(16)
    p, z, yh = slot // 8, (slot // 2) % 4, slot % 2
    angle = 2.0 * math.pi * ((kx[:, None] * (8 * z + yh * 2 + p)[None]) % 32) / 32
    cosine, sine = np.cos(angle), np.sin(angle)
    table = np.zeros((4, 2, 2, KX, 16, 4, 2, 2))
    for block in range(4):
        for k in range(2):
            table[block, 0, k, :, :, block, 0, k] = cosine
            table[block, 0, k, :, :, block, 1, k] = sine
            table[block, 1, k, :, :, block, 1, k] = cosine
            table[block, 1, k, :, :, block, 0, k] = -sine
    return table.reshape(512, 256).astype(ml_dtypes.bfloat16)


def forward_twiddle():
    kx = freq(np.arange(KX), KX)
    scale = 1.0 / math.sqrt(XCELLS * PLANE)
    place = np.arange(4)
    offset = (place // 2) * 128 + (place % 2) * 16
    lanes = np.arange(ROWS) // GROUP
    angle = 2.0 * math.pi * ((kx[None, :, None] * (offset[:, None, None] + lanes)) % XCELLS) / XCELLS
    return (np.stack([np.cos(angle), np.sin(angle)], axis=1) * scale).astype(np.float32)


def inverse_x_table():
    kx = freq(np.arange(KX), KX)
    angle = 2.0 * math.pi * ((kx[None] * (4 * np.arange(256))[:, None]) % XCELLS) / XCELLS
    cosine, sine = np.cos(angle), np.sin(angle)
    table = np.zeros((256, 2, 2, 2, 2, KX))
    for k in range(2):
        table[:, 0, k, 0, k] = cosine
        table[:, 0, k, 1, k] = -sine
        table[:, 1, k, 0, k] = sine
        table[:, 1, k, 1, k] = cosine
    return table.reshape(1024, 128).astype(ml_dtypes.bfloat16)


def inverse_twiddle():
    kx = np.tile(freq(np.arange(KX), KX), 2)
    kt2 = np.repeat(np.arange(2), KX)
    lanes = np.arange(128) // GROUP
    angle = 2.0 * math.pi * ((kx[:, None] * lanes[None]) % XCELLS) / XCELLS
    parts = np.stack([np.cos(angle), np.sin(angle)])
    weight = np.stack([np.where(kt2 + 2 * other == 0, 1.0, 2.0) for other in range(2)])
    scale = 0.5 / math.sqrt(PLANE)
    return (parts[None] * weight[:, None, :, None] * scale).astype(np.float32)


def place_of(g):
    return g // 16, (g // 8) % 2, (g // 2) % 4, g % 2


def exchange_kernel(
    state, weight, gain, bias, table, fxt, ftw, ixt, itw, out, pre, tbuf,
    xbuf, wbuf, gain_v, bias_v, fxt_v, ftw_v, ixt_v, itw_v, wmix,
    send1, recv1, send2, recv2, modes, send3, recv3,
    tsem, xsem, csem, ssem, rsem,
):
    g = lax.axis_index("gx")
    col = lax.axis_index("col")
    z, xlo, y, core = place_of(g)

    def zy_partner(dz, dy):
        z2, y2 = (z + dz) % 4, (y + dy) % 4
        return z2 * 16 + xlo * 8 + y2 * 2 + core, (y2 % 2) * 8 + z2 * 2 + y2 // 2

    def near_partner(k):
        xlo2, core2, col2 = (xlo + k % 2) % 2, (core + (k // 2) % 2) % 2, (col + k // 4) % 2
        return z * 16 + xlo2 * 8 + y * 2 + core2, col2, xlo2 * 2 + core2

    def wait_bytes(ref, sem):
        pltpu.make_async_copy(ref, ref, sem).wait()

    table_loads = []
    for k in range(2):
        cols = pl.ds(k * PIECE, PIECE)
        table_loads.append(pltpu.make_async_copy(table.at[:, cols], tbuf.at[:, cols], tsem.at[k]))
    rest = pl.ds(QUARTER, QUARTER)
    table_loads.append(pltpu.make_async_copy(table.at[:, rest], tbuf.at[:, rest], tsem.at[2]))
    state_loads = {}
    for h in range(2):
        for k in range(PIECES):
            for s in range(2):
                rows, at = pl.ds(h * HALF, HALF), pl.ds(s * FOLD + k * PIECE, PIECE)
                state_loads[h, k, s] = pltpu.make_async_copy(
                    state.at[rows, at], xbuf.at[rows, at], xsem.at[(h * PIECES + k) * 2 + s]
                )
    for k in range(PIECES):
        if k < 2:
            table_loads[k].start()
        for s in range(2):
            state_loads[0, k, s].start()
    constants = [
        pltpu.make_async_copy(gain, gain_v, csem.at[0]),
        pltpu.make_async_copy(bias, bias_v, csem.at[1]),
        pltpu.make_async_copy(weight, wbuf, csem.at[2]),
        pltpu.make_async_copy(fxt, fxt_v, csem.at[3]),
        pltpu.make_async_copy(ftw.at[xlo * 2 + core], ftw_v, csem.at[4]),
        pltpu.make_async_copy(itw, itw_v, csem.at[5]),
        pltpu.make_async_copy(ixt, ixt_v, csem.at[6]),
        table_loads[2],
    ]

    barrier = pltpu.get_barrier_semaphore()

    @pl.loop(1, 64)
    def _(k):
        pl.semaphore_signal(barrier, inc=1, device_id=((g + k) % 64, col), device_id_type=MESH)

    @pl.loop(4, 8)
    def _(k):
        to, col2, _slot = near_partner(k)
        pl.semaphore_signal(barrier, inc=1, device_id=(to, col2), device_id_type=MESH)

    row4 = lax.broadcasted_iota(jnp.int32, (256, HALF), 0) % 4
    mine1 = (y % 2) * 8 + z * 2 + y // 2
    for h in range(2):
        rows = pl.ds(h * HALF, HALF)
        sums = [[None, None], [None, None]]
        for k in range(PIECES):
            lo = pl.ds(k * PIECE, PIECE)
            hi = pl.ds(FOLD + k * PIECE, PIECE)
            cols = pl.ds((k % 2) * PIECE, PIECE)
            if h == 0 and k < 2:
                table_loads[k].wait()
            for s in range(2):
                state_loads[h, k, s].wait()
                if h == 0:
                    state_loads[1, k, s].start()
            x0, x1 = xbuf[rows, lo], xbuf[rows, hi]
            for p, x in ((0, x0 + x1), (1, x0 - x1)):
                part = lax.dot_general(
                    tbuf[pl.ds(p * 256, 256), cols], x, NT, preferred_element_type=F32
                )
                before = sums[p][k // 2]
                sums[p][k // 2] = part if before is None else before + part
        swapped = jnp.where(row4 < 2, pltpu.roll(sums[1][1], 254, 0), -pltpu.roll(sums[1][1], 2, 0))
        for p, second in ((0, sums[0][1]), (1, swapped)):
            first = sums[p][0].reshape(8, 2, 16, HALF)
            second = second.reshape(8, 2, 16, HALF)
            even, odd = first[:, 0] + second[:, 0], first[:, 1] - second[:, 1]
            both = jnp.stack([even, odd], axis=1).astype(BF16).reshape(2, 8, 16, HALF)
            for c in range(2):
                send1[c, pl.ds(h * 16 + p * 8, 8)] = both[c]
        if h == 0:
            for copy in constants:
                copy.start()
            pl.semaphore_wait(barrier, 67)
        for c in range(2):
            for dz, dy in FAR_FIRST:
                to, slot = zy_partner(dz, dy)
                pltpu.make_async_remote_copy(
                    send1.at[c, h * 16 + slot], recv1.at[c, h * 16 + mine1], ssem.at[c], rsem.at[c],
                    device_id=(to, col), device_id_type=MESH,
                ).start()

            recv1[c, h * 16 + mine1] = send1[c, h * 16 + mine1]

    constants[2].wait()
    left = lax.broadcasted_iota(jnp.int32, (GROUP, 128), 1) < 64

    @pl.loop(0, 64)
    def _(i):
        wr, wi = wbuf[0, i].astype(F32), wbuf[1, i].astype(F32)
        wr2, wi2 = pltpu.roll(wr, 64, 1), pltpu.roll(wi, 64, 1)
        wmix[0, 0, i] = jnp.where(left, wr, wr2)
        wmix[0, 1, i] = jnp.where(left, -wi, wi2)
        wmix[1, 0, i] = jnp.where(left, wr2, wr)
        wmix[1, 1, i] = jnp.where(left, -wi2, wi)

    for copy in constants[3:5]:
        copy.wait()
    lane_c = lax.broadcasted_iota(jnp.int32, (GROUP, HALF), 1) % GROUP
    row_c = lax.broadcasted_iota(jnp.int32, (GROUP, HALF), 0)
    pick = jnp.where(lane_c == row_c, 1.0, 0.0).astype(BF16)

    mine2 = col * 4 + xlo * 2 + core
    for c in range(2):
        wait_bytes(recv1.at[c, pl.ds(0, 30)], rsem.at[c])
        total = [None] * 2
        for h in range(2):
            lanes = pl.ds(h * HALF, HALF)
            data = recv1[c, pl.ds(h * 16, 16)].reshape(256, HALF)
            cosine, sine = ftw_v[0, :, lanes], ftw_v[1, :, lanes]
            for two in range(2):
                part = jnp.dot(fxt_v[pl.ds(two * 256, 256), :], data, preferred_element_type=F32)
                part = part.reshape(2, 2, 2, KX, HALF)
                real, imag = part[:, 0], part[:, 1]
                turned = jnp.stack([
                    real * cosine + imag * sine,
                    imag * cosine - real * sine,
                ], axis=1).reshape(256, HALF).astype(BF16)
                summed = lax.dot_general(pick, turned, NT, preferred_element_type=F32)
                total[two] = summed if h == 0 else total[two] + summed
        for two in range(2):
            for block in range(2):
                send2[c, two * 2 + block] = total[two][:, block * 128:(block + 1) * 128].astype(BF16)

        for k in (4, 6, 5, 7, 1, 3, 2):
            to, col2, block = near_partner(k)
            pltpu.make_async_remote_copy(
                send2.at[c, block], recv2.at[c, mine2], ssem.at[2 + c], rsem.at[2 + c],
                device_id=(to, col2), device_id_type=MESH,
            ).start()

        recv2[c, mine2] = send2[c, xlo * 2 + core]

    for copy in constants[5:7]:
        copy.wait()
    mine3 = (y % 2) * 32 + (z * 2 + y // 2) * 4 + xlo * 2 + core
    for c in range(2):
        wait_bytes(recv2.at[c, pl.ds(0, 7)], rsem.at[2 + c])
        for half in range(2):
            sum4 = recv2[c, half * 4].astype(F32)
            for k in range(1, 4):
                sum4 += recv2[c, half * 4 + k].astype(F32)
            sum4 = sum4.astype(BF16).astype(F32)
            modes[0, pl.ds(half * GROUP, GROUP), :] = sum4
            modes[1, pl.ds(half * GROUP, GROUP), :] = pltpu.roll(sum4, 64, 1)

        def mix(step, mixed):
            rows = pl.ds(pl.multiple_of(step * 8, 8), 8)
            straight, crossed = modes[0, rows, :], modes[1, rows, :]
            for k in range(8):
                i = step * 8 + k
                mixed += wmix[c, 0, i] * straight[k:k + 1] + wmix[c, 1, i] * crossed[k:k + 1]
            return mixed

        mixed = lax.fori_loop(0, 8, mix, jnp.zeros((GROUP, 128), F32)).astype(BF16)
        spread = lax.dot_general(mixed, pick[:, 0:128], TN, preferred_element_type=F32)
        other = jnp.minimum(core + c, 1)
        cosine, sine = itw_v[other, 0], itw_v[other, 1]
        real, imag = spread[0:64], spread[64:128]
        turned = jnp.concatenate([
            real * cosine - imag * sine,
            real * sine + imag * cosine,
        ]).astype(BF16)
        for q in range(4):
            rows = jnp.dot(ixt_v[pl.ds(q * 256, 256), :], turned, preferred_element_type=F32)
            send3[c, pl.ds(q * 16, 16)] = rows.astype(BF16).reshape(16, 16, 128)

        def share(k):
            dz, dy = 2 + 3 * (k // 16), 2 + 3 * ((k // 4) % 4)
            dx, dcore = 1 - (k // 2) % 2, 1 - k % 2
            z2, y2, xlo2, core2 = (z + dz) % 4, (y + dy) % 4, (xlo + dx) % 2, (core + dcore) % 2
            to = z2 * 16 + xlo2 * 8 + y2 * 2 + core2
            pltpu.make_async_remote_copy(
                send3.at[c, to], recv3.at[c, mine3], ssem.at[4 + c], rsem.at[4 + c],
                device_id=(to, col), device_id_type=MESH,
            ).start()

        pl.loop(0, 43)(share)
        pl.loop(44, 64)(share)
        recv3[c, mine3] = send3[c, g]

    for copy in constants[:2] + constants[7:]:
        copy.wait()
    square = (GROUP, GROUP)
    diagonal = lax.broadcasted_iota(jnp.int32, square, 0) == lax.broadcasted_iota(jnp.int32, square, 1)

    def column(row):
        part = 0.5 * jnp.sum(jnp.where(diagonal, row, 0.0), axis=1, keepdims=True)
        return jnp.broadcast_to(part, (GROUP, PRE))

    gain_c, bias_c = column(gain_v[...]), column(bias_v[...])

    @pl.loop(0, XDEV)
    def _(x):
        rows = pl.ds(pl.multiple_of(x * GROUP, GROUP), GROUP)
        for at in range(0, PLANE, PRE):
            pre[rows, pl.ds(at, PRE)] = xbuf[rows, pl.ds(at, PRE)].astype(F32) * gain_c + bias_c

    for c in range(2):
        wait_bytes(send1.at[c, pl.ds(0, 30)], ssem.at[c])
        wait_bytes(recv2.at[c, pl.ds(0, 7)], ssem.at[2 + c])
    for c in range(2):
        wait_bytes(recv3.at[c, pl.ds(0, 63)], rsem.at[4 + c])
        out[c] = recv3[c]
    for c in range(2):
        wait_bytes(send3.at[c, pl.ds(0, 63)], ssem.at[4 + c])


def finish_kernel(slabs, pre, table, out, vals, obuf, evens, odds, osem):
    c1 = 2.0 * math.sqrt(2.0 / math.pi)
    c3 = 8.0 * 0.044715 * math.sqrt(2.0 / math.pi)

    def store(j):
        return [
            pltpu.make_async_copy(
                obuf.at[j % 2, s], out.at[:, pl.ds(s * FOLD + j * STEP, STEP)], osem.at[j % 2, s]
            )
            for s in range(2)
        ]

    def products(n):
        cols = pl.ds(n * BLOCK, BLOCK)
        evens[n % 2] = jnp.dot(vals[:, 0:256], table[0:256, cols], preferred_element_type=F32)
        odds[n % 2] = jnp.dot(vals[:, 256:512], table[256:512, cols], preferred_element_type=F32)

    upper = lax.broadcasted_iota(jnp.int32, (32, 8, 128), 1) < 4
    for c in range(2):
        for pair in range(2):
            both = slabs[c].astype(F32)[:, pair * 8:(pair + 1) * 8, :].reshape(32, 2, 8, 128)
            first, second = both[:, 0], both[:, 1]
            quarters = (
                jnp.where(upper, first, pltpu.roll(second, 4, 1)),
                jnp.where(upper, pltpu.roll(first, 4, 1), second),
            )
            for q in range(2):
                quarter = quarters[q].reshape(256, 128)
                rows = pl.ds((pair * 2 + q) * 128, 128)
                for p in range(2):
                    vals[rows, pl.ds(p * 256 + c * 128, 128)] = quarter[p * 128:(p + 1) * 128].T.astype(BF16)
    products(0)
    steps = FOLD // STEP
    for j in range(steps):
        if j >= 2:
            for copy in store(j - 2):
                copy.wait()
        for i in range(STEP // BLOCK):
            n = j * (STEP // BLOCK) + i
            if (n + 1) * BLOCK < FOLD:
                products(n + 1)
            for m in range(ROWS // MB):
                rows = pl.ds(m * MB, MB)
                even, odd = evens[n % 2, rows, :], odds[n % 2, rows, :]
                for s in range(2):
                    spectral = even + odd if s == 0 else even - odd
                    v = spectral + pre[rows, pl.ds(s * FOLD + n * BLOCK, BLOCK)]
                    u = v * (c1 + c3 * (v * v))
                    obuf[j % 2, s, rows, pl.ds(i * BLOCK, BLOCK)] = (v + v * jnp.tanh(u)).astype(BF16)
        for copy in store(j):
            copy.start()
    for j in (steps - 2, steps - 1):
        for copy in store(j):
            copy.wait()


def in_hbm(array):
    return pltpu.with_memory_space_constraint(array, pltpu.HBM)


def shards(state_field, spectral_weight, local_weight, channel_bias):
    anywhere = pl.BlockSpec(memory_space=pltpu.HBM)
    vmem = pl.BlockSpec(memory_space=pltpu.VMEM)
    slabs, pre, table_v = pl.pallas_call(
        exchange_kernel,
        out_shape=[
            jax.ShapeDtypeStruct((2, 64, 16, 128), BF16),
            jax.ShapeDtypeStruct((ROWS, PLANE), F32),
            jax.ShapeDtypeStruct((512, FOLD), BF16),
        ],
        in_specs=[anywhere] * 9,
        out_specs=[vmem] * 3,
        scratch_shapes=[
            pltpu.VMEM((ROWS, PLANE), BF16),
            pltpu.VMEM((2, 64, GROUP, 128), BF16),
            pltpu.VMEM((1, GROUP), F32),
            pltpu.VMEM((1, GROUP), F32),
            pltpu.VMEM((512, 256), BF16),
            pltpu.VMEM((2, KX, ROWS), F32),
            pltpu.VMEM((1024, 128), BF16),
            pltpu.VMEM((2, 2, 64, 128), F32),
            pltpu.VMEM((2, 2, 64, GROUP, 128), F32),
            pltpu.VMEM((2, 32, 16, HALF), BF16),
            pltpu.VMEM((2, 32, 16, HALF), BF16),
            pltpu.VMEM((2, 4, GROUP, 128), BF16),
            pltpu.VMEM((2, 8, GROUP, 128), BF16),
            pltpu.VMEM((2, 64, 128), F32),
            pltpu.VMEM((2, 64, 16, 128), BF16),
            pltpu.VMEM((2, 64, 16, 128), BF16),
            pltpu.SemaphoreType.DMA((3,)),
            pltpu.SemaphoreType.DMA((4 * PIECES,)),
            pltpu.SemaphoreType.DMA((7,)),
            pltpu.SemaphoreType.DMA((6,)),
            pltpu.SemaphoreType.DMA((6,)),
        ],
        compiler_params=pltpu.CompilerParams(
            collective_id=0, has_side_effects=True, vmem_limit_bytes=24 << 20
        ),
        name="exchange",
    )(
        in_hbm(state_field.reshape(ROWS, PLANE)),
        in_hbm(spectral_weight),
        in_hbm(local_weight.reshape(1, GROUP)),
        in_hbm(channel_bias.reshape(1, GROUP)),
        *[in_hbm(jnp.asarray(make())) for make in (
            plane_table, forward_x_table, forward_twiddle, inverse_x_table, inverse_twiddle
        )],
    )
    result = pl.pallas_call(
        finish_kernel,
        out_shape=jax.ShapeDtypeStruct((ROWS, PLANE), BF16),
        in_specs=[vmem] * 3,
        out_specs=anywhere,
        scratch_shapes=[
            pltpu.VMEM((ROWS, 512), BF16),
            pltpu.VMEM((2, 2, ROWS, STEP), BF16),
            pltpu.VMEM((2, ROWS, BLOCK), F32),
            pltpu.VMEM((2, ROWS, BLOCK), F32),
            pltpu.SemaphoreType.DMA((2, 2)),
        ],
        compiler_params=pltpu.CompilerParams(vmem_limit_bytes=16 << 20),
        name="finish",
    )(slabs, pre, table_v)
    return result.reshape(state_field.shape)


def solution(mesh):
    return jax.shard_map(
        shards,
        mesh=mesh,
        in_specs=(P("gx", "col", None), P(None, None, "col", "gx"), P("col"), P("col")),
        out_specs=P("gx", "col", None),
        check_vma=False,
    )
```

time: 44.1 us -> 40.8 us (0.925)
  Pallas kernels: 44 us -> 40.7 us
    pallas_call x1, Pallas kernels: 35.8 us -> 32.5 us  [shards(): pl.pallas_call(exchange_kernel, out_shape=[jax.ShapeDtypeStruct((2, 64, 1...]
where the time goes in v3:
time: 40.8 us; the launch traced here: 40.7 us
  Pallas kernels  40.7 us (100%)
    pallas_call x1, Pallas kernels, shards(): pl.pallas_call(exchange_kernel, out_shape=[jax.ShapeDtypeStruct((2, 64, 1...  32.5 us
    pallas_call x1, Pallas kernels, shards(): pl.pallas_call(finish_kernel, out_shape=jax.ShapeDtypeStruct((ROWS, PLANE...  8.28 us

profile of v3, /device:TPU:1, one launch (start us, length us, event | category | flops | bytes accessed | tf_op | source)
XLA Modules:
  0.0 40.7 jit_solution(18090743493247497631)
XLA Ops:
  0.0 32.5 %exchange.1 = (bf16[2,64,16,128]{3,2,1,0:T(8,128)(2,1)S(1)}, f32[512,8192]{1,0:T(8,128)S(1)}, bf16[512,4096]{1,0:T(8,128)(2,1)S(1)}) custom-call(bf16[512,8192]{1,0:T(8,128)(2,1)} %bitcast.4, bf16[2,64,32,128]{3,2,1,0:T(8,128)(2,1)} %weight.1, f32[1,32]{1,0:T(1,128)} %bitcast.5, f32[1,32]{1,0:T(1,128)} %bitcast.6, bf16[512,4096]{1,0:T(8,128)(2,1)} %constant.10.clone.table, ...), custom_call_target="tpu_custom_call" | custom-call | tf_op jit(solution)/shard_map/exchange/pallas_call | solution.py:411
  32.5 8.3 %finish.1 = bf16[512,8192]{1,0:T(8,128)(2,1)} custom-call(bf16[2,64,16,128]{3,2,1,0:T(8,128)(2,1)S(1)} %get-tuple-element.8.slabs, f32[512,8192]{1,0:T(8,128)S(1)} %get-tuple-element.9.pre, bf16[512,4096]{1,0:T(8,128)(2,1)S(1)} %get-tuple-element.10.table), custom_call_target="tpu_custom_call" | custom-call | tf_op jit(solution)/shard_map/finish/pallas_call | solution.py:456

commit v4 on v3

--- a/solution.py
+++ b/solution.py
@@ -47,8 +47,8 @@
 
 
 def plane_table():
-    p, c, z, yh, xlo, half, r, kt2 = np.meshgrid(
-        *[np.arange(n) for n in (2, 2, 4, 2, 2, 2, 2, 2)], indexing="ij"
+    p, z, yh, c, xlo, half, r, kt2 = np.meshgrid(
+        *[np.arange(n) for n in (2, 4, 2, 2, 2, 2, 2, 2)], indexing="ij"
     )
     ky = freq((z * 8 + xlo * 4 + yh * 2 + p).reshape(-1), KY)
     kt = (half * 4 + c * 2 + kt2).reshape(-1)
@@ -89,36 +89,69 @@
 
 def inverse_x_table():
     kx = freq(np.arange(KX), KX)
-    angle = 2.0 * math.pi * ((kx[None] * (4 * np.arange(256))[:, None]) % XCELLS) / XCELLS
+    start = np.arange(2)[:, None] * 8 + np.arange(32)[None] * 32
+    angle = 2.0 * math.pi * ((kx * start[..., None]) % XCELLS) / XCELLS
     cosine, sine = np.cos(angle), np.sin(angle)
-    table = np.zeros((256, 2, 2, 2, 2, KX))
-    for k in range(2):
-        table[:, 0, k, 0, k] = cosine
-        table[:, 0, k, 1, k] = -sine
-        table[:, 1, k, 0, k] = sine
-        table[:, 1, k, 1, k] = cosine
-    return table.reshape(1024, 128).astype(ml_dtypes.bfloat16)
+    table = np.zeros((2, 32, 2, 2, 2, 2, 2, 2, KX))
+    for core in range(2):
+        for k in range(2):
+            table[:, :, core, 0, k, core, 0, k] = cosine
+            table[:, :, core, 0, k, core, 1, k] = -sine
+            table[:, :, core, 1, k, core, 0, k] = sine
+            table[:, :, core, 1, k, core, 1, k] = cosine
+    return table.reshape(2, 256, 256).astype(ml_dtypes.bfloat16)
 
 
 def inverse_twiddle():
     kx = np.tile(freq(np.arange(KX), KX), 2)
     kt2 = np.repeat(np.arange(2), KX)
-    lanes = np.arange(128) // GROUP
-    angle = 2.0 * math.pi * ((kx[:, None] * lanes[None]) % XCELLS) / XCELLS
-    parts = np.stack([np.cos(angle), np.sin(angle)])
+    lanes = np.arange(2)[:, None] * XDEV + np.arange(HALF)[None] // GROUP
+    angle = 2.0 * math.pi * ((kx[None, :, None] * lanes[:, None]) % XCELLS) / XCELLS
+    parts = np.stack([np.cos(angle), np.sin(angle)], axis=1)
     weight = np.stack([np.where(kt2 + 2 * other == 0, 1.0, 2.0) for other in range(2)])
     scale = 0.5 / math.sqrt(PLANE)
-    return (parts[None] * weight[:, None, :, None] * scale).astype(np.float32)
+    return (parts[:, None] * weight[None, :, None, :, None] * scale).astype(np.float32)
 
 
 def place_of(g):
     return g // 16, (g // 8) % 2, (g // 2) % 4, g % 2
 
 
+def arrange(shares, vals):
+    tiles = shares.astype(F32).reshape(16, 2, 2, 8, HALF)
+    tiles = jnp.stack([tiles[:, 0, 0], tiles[:, 1, 0], tiles[:, 0, 1], tiles[:, 1, 1]], axis=1)
+    vals[...] = tiles.reshape(512, HALF).T.astype(BF16)
+
+
+def transform_back(vals, pre, table, evens, odds, put, after):
+    c1 = 2.0 * math.sqrt(2.0 / math.pi)
+    c3 = 8.0 * 0.044715 * math.sqrt(2.0 / math.pi)
+
+    def products(n):
+        cols = pl.ds(n * BLOCK, BLOCK)
+        evens[n % 2] = jnp.dot(vals[:, 0:256], table[0:256, cols], preferred_element_type=F32)
+        odds[n % 2] = jnp.dot(vals[:, 256:512], table[256:512, cols], preferred_element_type=F32)
+
+    products(0)
+    for n in range(FOLD // BLOCK):
+        if (n + 1) * BLOCK < FOLD:
+            products(n + 1)
+        for m in range(HALF // MB):
+            rows = pl.ds(m * MB, MB)
+            even, odd = evens[n % 2, rows, :], odds[n % 2, rows, :]
+            for s in range(2):
+                spectral = even + odd if s == 0 else even - odd
+                v = spectral + pre[rows, pl.ds(s * FOLD + n * BLOCK, BLOCK)]
+                u = v * (c1 + c3 * (v * v))
+                put(n, s, rows, (v + v * jnp.tanh(u)).astype(BF16))
+        after(n)
+
+
 def exchange_kernel(
-    state, weight, gain, bias, table, fxt, ftw, ixt, itw, out, pre, tbuf,
+    state, weight, gain, bias, table, fxt, ftw, ixt, itw, out, shares, pre1, tbuf,
     xbuf, wbuf, gain_v, bias_v, fxt_v, ftw_v, ixt_v, itw_v, wmix,
-    send1, recv1, send2, recv2, modes, send3, recv3,
+    send1, recv1, send2, recv2, modes, own, near, turned_v, send3, recv3,
+    pre0, vals, evens, odds,
     tsem, xsem, csem, ssem, rsem,
 ):
     g = lax.axis_index("gx")
@@ -161,7 +194,7 @@
         pltpu.make_async_copy(weight, wbuf, csem.at[2]),
         pltpu.make_async_copy(fxt, fxt_v, csem.at[3]),
         pltpu.make_async_copy(ftw.at[xlo * 2 + core], ftw_v, csem.at[4]),
-        pltpu.make_async_copy(itw, itw_v, csem.at[5]),
+        pltpu.make_async_copy(itw.at[core], itw_v, csem.at[5]),
         pltpu.make_async_copy(ixt, ixt_v, csem.at[6]),
         table_loads[2],
     ]
@@ -201,12 +234,12 @@
                 sums[p][k // 2] = part if before is None else before + part
         swapped = jnp.where(row4 < 2, pltpu.roll(sums[1][1], 254, 0), -pltpu.roll(sums[1][1], 2, 0))
         for p, second in ((0, sums[0][1]), (1, swapped)):
-            first = sums[p][0].reshape(8, 2, 16, HALF)
-            second = second.reshape(8, 2, 16, HALF)
+            first = sums[p][0].reshape(4, 2, 32, HALF)
+            second = second.reshape(4, 2, 32, HALF)
             even, odd = first[:, 0] + second[:, 0], first[:, 1] - second[:, 1]
-            both = jnp.stack([even, odd], axis=1).astype(BF16).reshape(2, 8, 16, HALF)
+            both = jnp.stack([even, odd], axis=1).astype(BF16).reshape(8, 2, 16, HALF)
             for c in range(2):
-                send1[c, pl.ds(h * 16 + p * 8, 8)] = both[c]
+                send1[c, pl.ds(h * 16 + p * 8, 8)] = both[:, c]
         if h == 0:
             for copy in constants:
                 copy.start()
@@ -272,7 +305,17 @@
 
     for copy in constants[5:7]:
         copy.wait()
-    mine3 = (y % 2) * 32 + (z * 2 + y // 2) * 4 + xlo * 2 + core
+
+    def turn(mixed, of, c):
+        spread = lax.dot_general(mixed, pick, TN, preferred_element_type=F32)
+        other = jnp.minimum(of + c, 1)
+        cosine, sine = itw_v[other, 0], itw_v[other, 1]
+        real, imag = spread[0:64], spread[64:128]
+        turned_v[c, of] = jnp.concatenate([
+            real * cosine - imag * sine,
+            real * sine + imag * cosine,
+        ]).astype(BF16)
+
     for c in range(2):
         wait_bytes(recv2.at[c, pl.ds(0, 7)], rsem.at[2 + c])
         for half in range(2):
@@ -291,32 +334,36 @@
                 mixed += wmix[c, 0, i] * straight[k:k + 1] + wmix[c, 1, i] * crossed[k:k + 1]
             return mixed
 
-        mixed = lax.fori_loop(0, 8, mix, jnp.zeros((GROUP, 128), F32)).astype(BF16)
-        spread = lax.dot_general(mixed, pick[:, 0:128], TN, preferred_element_type=F32)
-        other = jnp.minimum(core + c, 1)
-        cosine, sine = itw_v[other, 0], itw_v[other, 1]
-        real, imag = spread[0:64], spread[64:128]
-        turned = jnp.concatenate([
-            real * cosine - imag * sine,
-            real * sine + imag * cosine,
-        ]).astype(BF16)
-        for q in range(4):
-            rows = jnp.dot(ixt_v[pl.ds(q * 256, 256), :], turned, preferred_element_type=F32)
-            send3[c, pl.ds(q * 16, 16)] = rows.astype(BF16).reshape(16, 16, 128)
+        own[c] = lax.fori_loop(0, 8, mix, jnp.zeros((GROUP, 128), F32)).astype(BF16)
+        pltpu.make_async_remote_copy(
+            own.at[c], near.at[c], ssem.at[4 + c], rsem.at[4 + c],
+            device_id=(g + 1 - 2 * core, col), device_id_type=MESH,
+        ).start()
+        turn(own[c], core, c)
+    for c in range(2):
+        wait_bytes(near.at[c], rsem.at[4 + c])
+        turn(near[c], 1 - core, c)
+
+    chip = z * 8 + xlo * 4 + y
+    mine3 = (y % 2) * 16 + z * 4 + (y // 2) * 2 + xlo
+    for half in range(2):
+        tiles = [
+            jnp.dot(ixt_v[half], turned_v[c].reshape(256, HALF), preferred_element_type=F32).reshape(32, 8, HALF)
+            for c in range(2)
+        ]
+        send3[half] = jnp.concatenate(tiles, axis=1).astype(BF16)
 
         def share(k):
-            dz, dy = 2 + 3 * (k // 16), 2 + 3 * ((k // 4) % 4)
-            dx, dcore = 1 - (k // 2) % 2, 1 - k % 2
-            z2, y2, xlo2, core2 = (z + dz) % 4, (y + dy) % 4, (xlo + dx) % 2, (core + dcore) % 2
-            to = z2 * 16 + xlo2 * 8 + y2 * 2 + core2
+            z2, y2 = (z + 2 + 3 * (k // 8)) % 4, (y + 2 + 3 * ((k // 2) % 4)) % 4
+            to = z2 * 8 + ((xlo + 1 - k % 2) % 2) * 4 + y2
             pltpu.make_async_remote_copy(
-                send3.at[c, to], recv3.at[c, mine3], ssem.at[4 + c], rsem.at[4 + c],
-                device_id=(to, col), device_id_type=MESH,
+                send3.at[half, to], recv3.at[half, mine3], ssem.at[6 + half], rsem.at[6 + half],
+                device_id=(to * 2 + core, col), device_id_type=MESH,
             ).start()
 
-        pl.loop(0, 43)(share)
-        pl.loop(44, 64)(share)
-        recv3[c, mine3] = send3[c, g]
+        pl.loop(0, 21)(share)
+        pl.loop(22, 32)(share)
+        recv3[half, mine3] = send3[half, chip]
 
     for copy in constants[:2] + constants[7:]:
         copy.wait()
@@ -329,76 +376,54 @@
 
     gain_c, bias_c = column(gain_v[...]), column(bias_v[...])
 
-    @pl.loop(0, XDEV)
-    def _(x):
-        rows = pl.ds(pl.multiple_of(x * GROUP, GROUP), GROUP)
-        for at in range(0, PLANE, PRE):
-            pre[rows, pl.ds(at, PRE)] = xbuf[rows, pl.ds(at, PRE)].astype(F32) * gain_c + bias_c
+    for half, pre in ((0, pre0), (1, pre1)):
+        @pl.loop(0, XDEV // 2)
+        def _(x):
+            start = pl.multiple_of(x * GROUP, GROUP)
+            for at in range(0, PLANE, PRE):
+                cells = xbuf[pl.ds(start + half * HALF, GROUP), pl.ds(at, PRE)].astype(F32)
+                pre[pl.ds(start, GROUP), pl.ds(at, PRE)] = cells * gain_c + bias_c
 
     for c in range(2):
         wait_bytes(send1.at[c, pl.ds(0, 30)], ssem.at[c])
         wait_bytes(recv2.at[c, pl.ds(0, 7)], ssem.at[2 + c])
-    for c in range(2):
-        wait_bytes(recv3.at[c, pl.ds(0, 63)], rsem.at[4 + c])
-        out[c] = recv3[c]
-    for c in range(2):
-        wait_bytes(send3.at[c, pl.ds(0, 63)], ssem.at[4 + c])
-
-
-def finish_kernel(slabs, pre, table, out, vals, obuf, evens, odds, osem):
-    c1 = 2.0 * math.sqrt(2.0 / math.pi)
-    c3 = 8.0 * 0.044715 * math.sqrt(2.0 / math.pi)
-
-    def store(j):
-        return [
-            pltpu.make_async_copy(
-                obuf.at[j % 2, s], out.at[:, pl.ds(s * FOLD + j * STEP, STEP)], osem.at[j % 2, s]
-            )
-            for s in range(2)
-        ]
-
-    def products(n):
-        cols = pl.ds(n * BLOCK, BLOCK)
-        evens[n % 2] = jnp.dot(vals[:, 0:256], table[0:256, cols], preferred_element_type=F32)
-        odds[n % 2] = jnp.dot(vals[:, 256:512], table[256:512, cols], preferred_element_type=F32)
-
-    upper = lax.broadcasted_iota(jnp.int32, (32, 8, 128), 1) < 4
-    for c in range(2):
-        for pair in range(2):
-            both = slabs[c].astype(F32)[:, pair * 8:(pair + 1) * 8, :].reshape(32, 2, 8, 128)
-            first, second = both[:, 0], both[:, 1]
-            quarters = (
-                jnp.where(upper, first, pltpu.roll(second, 4, 1)),
-                jnp.where(upper, pltpu.roll(first, 4, 1), second),
-            )
-            for q in range(2):
-                quarter = quarters[q].reshape(256, 128)
-                rows = pl.ds((pair * 2 + q) * 128, 128)
-                for p in range(2):
-                    vals[rows, pl.ds(p * 256 + c * 128, 128)] = quarter[p * 128:(p + 1) * 128].T.astype(BF16)
-    products(0)
-    steps = FOLD // STEP
-    for j in range(steps):
-        if j >= 2:
-            for copy in store(j - 2):
-                copy.wait()
-        for i in range(STEP // BLOCK):
-            n = j * (STEP // BLOCK) + i
-            if (n + 1) * BLOCK < FOLD:
-                products(n + 1)
-            for m in range(ROWS // MB):
-                rows = pl.ds(m * MB, MB)
-                even, odd = evens[n % 2, rows, :], odds[n % 2, rows, :]
-                for s in range(2):
-                    spectral = even + odd if s == 0 else even - odd
-                    v = spectral + pre[rows, pl.ds(s * FOLD + n * BLOCK, BLOCK)]
-                    u = v * (c1 + c3 * (v * v))
-                    obuf[j % 2, s, rows, pl.ds(i * BLOCK, BLOCK)] = (v + v * jnp.tanh(u)).astype(BF16)
-        for copy in store(j):
-            copy.start()
-    for j in (steps - 2, steps - 1):
-        for copy in store(j):
-            copy.wait()
+        wait_bytes(own.at[c], ssem.at[4 + c])
+
+    def put(n, s, rows, values):
+        out[rows, pl.ds(s * FOLD + n * BLOCK, BLOCK)] = values
+
+    wait_bytes(recv3.at[0, pl.ds(0, 31)], rsem.at[6])
+    arrange(recv3[0], vals)
+    transform_back(vals, pre0, tbuf, evens, odds, put, lambda n: None)
+    wait_bytes(recv3.at[1, pl.ds(0, 31)], rsem.at[7])
+    shares[...] = recv3[1]
+    for half in range(2):
+        wait_bytes(send3.at[half, pl.ds(0, 31)], ssem.at[6 + half])
+
+
+def finish_kernel(first, shares, pre, table, out, vals, obuf, evens, odds, fsem, osem):
+    per = STEP // BLOCK
+
+    def store(j, s):
+        cols = pl.ds(s * FOLD + j * STEP, STEP)
+        return pltpu.make_async_copy(obuf.at[:, cols], out.at[pl.ds(HALF, HALF), cols], osem.at[j, s])
+
+    def put(n, s, rows, values):
+        obuf[rows, pl.ds(s * FOLD + n * BLOCK, BLOCK)] = values
+
+    def after(n):
+        if n % per == per - 1:
+            store(n // per, 0).start()
+            store(n // per, 1).start()
+
+    first_half = pltpu.make_async_copy(first, out.at[pl.ds(0, HALF), :], fsem)
+    first_half.start()
+    arrange(shares[...], vals)
+    transform_back(vals, pre, table, evens, odds, put, after)
+    for j in range(FOLD // STEP):
+        store(j, 0).wait()
+        store(j, 1).wait()
+    first_half.wait()
 
 
 def in_hbm(array):
@@ -408,15 +433,16 @@
 def shards(state_field, spectral_weight, local_weight, channel_bias):
     anywhere = pl.BlockSpec(memory_space=pltpu.HBM)
     vmem = pl.BlockSpec(memory_space=pltpu.VMEM)
-    slabs, pre, table_v = pl.pallas_call(
+    first, shares, pre, table_v = pl.pallas_call(
         exchange_kernel,
         out_shape=[
-            jax.ShapeDtypeStruct((2, 64, 16, 128), BF16),
-            jax.ShapeDtypeStruct((ROWS, PLANE), F32),
+            jax.ShapeDtypeStruct((HALF, PLANE), BF16),
+            jax.ShapeDtypeStruct((32, 16, HALF), BF16),
+            jax.ShapeDtypeStruct((HALF, PLANE), F32),
             jax.ShapeDtypeStruct((512, FOLD), BF16),
         ],
         in_specs=[anywhere] * 9,
-        out_specs=[vmem] * 3,
+        out_specs=[vmem] * 4,
         scratch_shapes=[
             pltpu.VMEM((ROWS, PLANE), BF16),
             pltpu.VMEM((2, 64, GROUP, 128), BF16),
@@ -424,24 +450,31 @@
             pltpu.VMEM((1, GROUP), F32),
             pltpu.VMEM((512, 256), BF16),
             pltpu.VMEM((2, KX, ROWS), F32),
-            pltpu.VMEM((1024, 128), BF16),
-            pltpu.VMEM((2, 2, 64, 128), F32),
+            pltpu.VMEM((2, 256, 256), BF16),
+            pltpu.VMEM((2, 2, 64, HALF), F32),
             pltpu.VMEM((2, 2, 64, GROUP, 128), F32),
             pltpu.VMEM((2, 32, 16, HALF), BF16),
             pltpu.VMEM((2, 32, 16, HALF), BF16),
             pltpu.VMEM((2, 4, GROUP, 128), BF16),
             pltpu.VMEM((2, 8, GROUP, 128), BF16),
             pltpu.VMEM((2, 64, 128), F32),
-            pltpu.VMEM((2, 64, 16, 128), BF16),
-            pltpu.VMEM((2, 64, 16, 128), BF16),
+            pltpu.VMEM((2, GROUP, 128), BF16),
+            pltpu.VMEM((2, GROUP, 128), BF16),
+            pltpu.VMEM((2, 2, 128, HALF), BF16),
+            pltpu.VMEM((2, 32, 16, HALF), BF16),
+            pltpu.VMEM((2, 32, 16, HALF), BF16),
+            pltpu.VMEM((HALF, PLANE), F32),
+            pltpu.VMEM((HALF, 512), BF16),
+            pltpu.VMEM((2, HALF, BLOCK), F32),
+            pltpu.VMEM((2, HALF, BLOCK), F32),
             pltpu.SemaphoreType.DMA((3,)),
             pltpu.SemaphoreType.DMA((4 * PIECES,)),
             pltpu.SemaphoreType.DMA((7,)),
-            pltpu.SemaphoreType.DMA((6,)),
-            pltpu.SemaphoreType.DMA((6,)),
+            pltpu.SemaphoreType.DMA((8,)),
+            pltpu.SemaphoreType.DMA((8,)),
         ],
         compiler_params=pltpu.CompilerParams(
-            collective_id=0, has_side_effects=True, vmem_limit_bytes=24 << 20
+            collective_id=0, has_side_effects=True, vmem_limit_bytes=32 << 20
         ),
         name="exchange",
     )(
@@ -456,18 +489,19 @@
     result = pl.pallas_call(
         finish_kernel,
         out_shape=jax.ShapeDtypeStruct((ROWS, PLANE), BF16),
-        in_specs=[vmem] * 3,
+        in_specs=[vmem] * 4,
         out_specs=anywhere,
         scratch_shapes=[
-            pltpu.VMEM((ROWS, 512), BF16),
-            pltpu.VMEM((2, 2, ROWS, STEP), BF16),
-            pltpu.VMEM((2, ROWS, BLOCK), F32),
-            pltpu.VMEM((2, ROWS, BLOCK), F32),
-            pltpu.SemaphoreType.DMA((2, 2)),
+            pltpu.VMEM((HALF, 512), BF16),
+            pltpu.VMEM((HALF, PLANE), BF16),
+            pltpu.VMEM((2, HALF, BLOCK), F32),
+            pltpu.VMEM((2, HALF, BLOCK), F32),
+            pltpu.SemaphoreType.DMA,
+            pltpu.SemaphoreType.DMA((FOLD // STEP, 2)),
         ],
         compiler_params=pltpu.CompilerParams(vmem_limit_bytes=16 << 20),
         name="finish",
-    )(slabs, pre, table_v)
+    )(first, shares, pre, table_v)
     return result.reshape(state_field.shape)
 
 

time: 40.8 us -> 38.2 us (0.936)
  Pallas kernels: 40.7 us -> 38.1 us
    pallas_call x1, Pallas kernels: 8.28 us -> 4.2 us  [shards(): pl.pallas_call(finish_kernel, out_shape=jax.ShapeDtypeStruct((ROWS, PLANE...]
    pallas_call x1, Pallas kernels: 32.5 us -> 33.9 us  [shards(): pl.pallas_call(exchange_kernel, out_shape=[jax.ShapeDtypeStruct((HALF, PL...]
where the time goes in v4:
time: 38.2 us; the launch traced here: 38.1 us
  Pallas kernels  38.1 us (100%)
    pallas_call x1, Pallas kernels, shards(): pl.pallas_call(exchange_kernel, out_shape=[jax.ShapeDtypeStruct((HALF, PL...  33.9 us
    pallas_call x1, Pallas kernels, shards(): pl.pallas_call(finish_kernel, out_shape=jax.ShapeDtypeStruct((ROWS, PLANE...  4.2 us

profile of v4, /device:TPU:1, one launch (start us, length us, event | category | flops | bytes accessed | tf_op | source)
XLA Modules:
  0.0 38.1 jit_solution(11609827016833606409)
XLA Ops:
  0.0 33.9 %exchange.1 = (bf16[256,8192]{1,0:T(8,128)(2,1)S(1)}, bf16[32,16,256]{2,1,0:T(8,128)(2,1)S(1)}, f32[256,8192]{1,0:T(8,128)S(1)}, bf16[512,4096]{1,0:T(8,128)(2,1)S(1)}) custom-call(bf16[512,8192]{1,0:T(8,128)(2,1)} %bitcast.4, bf16[2,64,32,128]{3,2,1,0:T(8,128)(2,1)} %weight.1, f32[1,32]{1,0:T(1,128)} %bitcast.5, f32[1,32]{1,0:T(1,128)} %bitcast.6, ...), custom_call_target="tpu_custom_call" | custom-call | tf_op jit(solution)/shard_map/exchange/pallas_call | solution.py:436
  33.9 4.2 %finish.1 = bf16[512,8192]{1,0:T(8,128)(2,1)} custom-call(bf16[256,8192]{1,0:T(8,128)(2,1)S(1)} %get-tuple-element.9.first, bf16[32,16,256]{2,1,0:T(8,128)(2,1)S(1)} %get-tuple-element.10.shares, f32[256,8192]{1,0:T(8,128)S(1)} %get-tuple-element.11.pre, bf16[512,4096]{1,0:T(8,128)(2,1)S(1)} %get-tuple-element.12.table), custom_call_target="tpu_custom_call" | custom-call | tf_op jit(solution)/shard_map/finish/pallas_call | solution.py:489

commit v5 on v4

--- a/solution.py
+++ b/solution.py
@@ -201,11 +201,12 @@
 
     barrier = pltpu.get_barrier_semaphore()
 
-    @pl.loop(1, 64)
+    @pl.loop(1, 32)
     def _(k):
-        pl.semaphore_signal(barrier, inc=1, device_id=((g + k) % 64, col), device_id_type=MESH)
-
-    @pl.loop(4, 8)
+        to = (g + 2 * k) % 64
+        pl.semaphore_signal(barrier, inc=1, device_id=(to, col), device_id_type=MESH)
+
+    @pl.loop(2, 8)
     def _(k):
         to, col2, _slot = near_partner(k)
         pl.semaphore_signal(barrier, inc=1, device_id=(to, col2), device_id_type=MESH)
@@ -243,7 +244,7 @@
         if h == 0:
             for copy in constants:
                 copy.start()
-            pl.semaphore_wait(barrier, 67)
+            pl.semaphore_wait(barrier, 37)
         for c in range(2):
             for dz, dy in FAR_FIRST:
                 to, slot = zy_partner(dz, dy)

time: 38.2 us -> 38.1 us (level)
  no operation moved by 1% of the time
where the time goes in v5:
time: 38.1 us; the launch traced here: 37.9 us
  Pallas kernels  37.9 us (99%)
    pallas_call x1, Pallas kernels, shards(): pl.pallas_call(exchange_kernel, out_shape=[jax.ShapeDtypeStruct((HALF, PL...  33.7 us
    pallas_call x1, Pallas kernels, shards(): pl.pallas_call(finish_kernel, out_shape=jax.ShapeDtypeStruct((ROWS, PLANE...  4.2 us

profile of v5, /device:TPU:1, one launch (start us, length us, event | category | flops | bytes accessed | tf_op | source)
XLA Modules:
  0.0 37.9 jit_solution(7838062505970776917)
XLA Ops:
  0.0 33.7 %exchange.1 = (bf16[256,8192]{1,0:T(8,128)(2,1)S(1)}, bf16[32,16,256]{2,1,0:T(8,128)(2,1)S(1)}, f32[256,8192]{1,0:T(8,128)S(1)}, bf16[512,4096]{1,0:T(8,128)(2,1)S(1)}) custom-call(bf16[512,8192]{1,0:T(8,128)(2,1)} %bitcast.4, bf16[2,64,32,128]{3,2,1,0:T(8,128)(2,1)} %weight.1, f32[1,32]{1,0:T(1,128)} %bitcast.5, f32[1,32]{1,0:T(1,128)} %bitcast.6, ...), custom_call_target="tpu_custom_call" | custom-call | tf_op jit(solution)/shard_map/exchange/pallas_call | solution.py:437
  33.7 4.2 %finish.1 = bf16[512,8192]{1,0:T(8,128)(2,1)} custom-call(bf16[256,8192]{1,0:T(8,128)(2,1)S(1)} %get-tuple-element.9.first, bf16[32,16,256]{2,1,0:T(8,128)(2,1)S(1)} %get-tuple-element.10.shares, f32[256,8192]{1,0:T(8,128)S(1)} %get-tuple-element.11.pre, bf16[512,4096]{1,0:T(8,128)(2,1)S(1)} %get-tuple-element.12.table), custom_call_target="tpu_custom_call" | custom-call | tf_op jit(solution)/shard_map/finish/pallas_call | solution.py:490

commit v6 on v5

--- a/solution.py
+++ b/solution.py
@@ -417,14 +417,18 @@
             store(n // per, 0).start()
             store(n // per, 1).start()
 
-    first_half = pltpu.make_async_copy(first, out.at[pl.ds(0, HALF), :], fsem)
-    first_half.start()
+    first_half = []
+    for k in range(4):
+        rows = pl.ds(k * MB, MB)
+        first_half.append(pltpu.make_async_copy(first.at[rows, :], out.at[rows, :], fsem.at[k]))
+        first_half[-1].start()
     arrange(shares[...], vals)
     transform_back(vals, pre, table, evens, odds, put, after)
     for j in range(FOLD // STEP):
         store(j, 0).wait()
         store(j, 1).wait()
-    first_half.wait()
+    for copy in first_half:
+        copy.wait()
 
 
 def in_hbm(array):
@@ -497,7 +501,7 @@
             pltpu.VMEM((HALF, PLANE), BF16),
             pltpu.VMEM((2, HALF, BLOCK), F32),
             pltpu.VMEM((2, HALF, BLOCK), F32),
-            pltpu.SemaphoreType.DMA,
+            pltpu.SemaphoreType.DMA((4,)),
             pltpu.SemaphoreType.DMA((FOLD // STEP, 2)),
         ],
         compiler_params=pltpu.CompilerParams(vmem_limit_bytes=16 << 20),

time: 38.1 us -> 38.1 us (level)
  no operation moved by 1% of the time
where the time goes in v6:
time: 38.1 us; the launch traced here: 37.9 us
  Pallas kernels  37.9 us (99%)
    pallas_call x1, Pallas kernels, shards(): pl.pallas_call(exchange_kernel, out_shape=[jax.ShapeDtypeStruct((HALF, PL...  33.7 us
    pallas_call x1, Pallas kernels, shards(): pl.pallas_call(finish_kernel, out_shape=jax.ShapeDtypeStruct((ROWS, PLANE...  4.23 us

profile of v6, /device:TPU:1, one launch (start us, length us, event | category | flops | bytes accessed | tf_op | source)
XLA Modules:
  0.0 37.9 jit_solution(16960642489314877560)
XLA Ops:
  0.0 33.7 %exchange.1 = (bf16[256,8192]{1,0:T(8,128)(2,1)S(1)}, bf16[32,16,256]{2,1,0:T(8,128)(2,1)S(1)}, f32[256,8192]{1,0:T(8,128)S(1)}, bf16[512,4096]{1,0:T(8,128)(2,1)S(1)}) custom-call(bf16[512,8192]{1,0:T(8,128)(2,1)} %bitcast.4, bf16[2,64,32,128]{3,2,1,0:T(8,128)(2,1)} %weight.1, f32[1,32]{1,0:T(1,128)} %bitcast.5, f32[1,32]{1,0:T(1,128)} %bitcast.6, ...), custom_call_target="tpu_custom_call" | custom-call | tf_op jit(solution)/shard_map/exchange/pallas_call | solution.py:441
  33.7 4.2 %finish.1 = bf16[512,8192]{1,0:T(8,128)(2,1)} custom-call(bf16[256,8192]{1,0:T(8,128)(2,1)S(1)} %get-tuple-element.9.first, bf16[32,16,256]{2,1,0:T(8,128)(2,1)S(1)} %get-tuple-element.10.shares, f32[256,8192]{1,0:T(8,128)S(1)} %get-tuple-element.11.pre, bf16[512,4096]{1,0:T(8,128)(2,1)S(1)} %get-tuple-element.12.table), custom_call_target="tpu_custom_call" | custom-call | tf_op jit(solution)/shard_map/finish/pallas_call | solution.py:494
